TPU v7x, 32 devices: a whole 2x2x4 slice. The times are simulated.
32 devices in a mesh: groups: 2 (over x), slab: 16 (over z, y, core).
Axes of the slice: x: 2, y: 2, z: 4, core: 2. Of those that a mesh axis runs over, the one named last changes fastest.
Arguments:
- volume: bfloat16 [64, 48, 48, 128], P(('groups', 'slab')), parts along dimension 0, may hold values from -6 to 6
- kernel: bfloat16 [3, 3, 3, 128, 128], replicated, may hold values from -0.109375 to 0.109375
- grad_out: bfloat16 [64, 48, 48, 128], P(('groups', 'slab')), parts along dimension 0, may hold values from -6 to 6
Outputs:
- activation: bfloat16 [64, 48, 48, 128], P(('groups', 'slab')), parts along dimension 0
- input_grad: bfloat16 [64, 48, 48, 128], P(('groups', 'slab')), parts along dimension 0
- weight_grad: float32 [6, 3, 3, 128, 128], P('groups'), parts along dimension 0
There are 2 independent parts, one for each index of `groups`. A program takes and returns all parts, laid end to end along the dimension named above; an argument that names none is the same for every part. Nothing has to cross between parts.
All inputs are finite; a program needn't handle non-finite values.
Results may differ from a plain program's by a relative error of at most 0.001.
Values may be sent and summed in bfloat16 or wider, within the bound.
A program may use at most 64 MiB of HBM per device.

v0:
```python
import functools

import jax
import jax.numpy as jnp
import numpy as np
from jax import lax
from jax.experimental import pallas as pl
from jax.experimental.pallas import tpu as pltpu
from jax.sharding import PartitionSpec as P

MESH = pl.DeviceIdType.MESH
F32 = jnp.float32
BF16 = jnp.bfloat16


def layer_kernel(
    n, line, cols, height, breadth, ch, tile, factor,
    vol, ker, grd,
    act_out, ing_out, dw_out,
    vp, gp, wf, wb, xt, gs, acc, fin, r_sib, r_lo, r_hi, r_y, act, ing,
    s_in, s_w, s_hs, s_hr, s_sib, r_sibs, s_line, r_los, r_his, s_y, r_ys,
    s_up, s_dn, s_fs, r_fin, r_fsib, s_out,
):
    cells = height * breadth
    half = ch // 2
    taps = 9
    me = lax.axis_index("slab")
    core = lax.rem(me, 2)
    chip = me // 2
    z = chip // cols
    y = lax.rem(chip, cols)
    sib = me + 1 - 2 * core
    zlo = me - 2 * cols
    zhi = me + 2 * cols
    has_lo, has_hi = z > 0, z < line - 1
    has_before, has_after = me > 0, me < n - 1

    def peer(k):
        return (z * cols + lax.rem(y + k, cols)) * 2 + core

    inner = pl.ds(breadth, cells)
    loads = []
    for p in range(2):
        loads.append(pltpu.make_async_copy(vol.at[p], vp.at[p + 1, inner], s_in.at[p]))
    for p in range(2):
        loads.append(pltpu.make_async_copy(grd.at[p], gp.at[p + 1, inner], s_in.at[p + 2]))
    for copy in loads:
        copy.start()
    wloads = []
    for a in range(3):
        for d in range(2):
            p = a + d
            wloads.append(pltpu.make_async_copy(
                ker.at[a], wf.at[:, :, pl.ds(p * ch, ch), pl.ds(d * ch, ch)], s_w.at[0, a, d]))
            p = d + 2 - a
            wloads.append(pltpu.make_async_copy(
                ker.at[a], wb.at[:, :, pl.ds(d * ch, ch), pl.ds(p * ch, ch)], s_w.at[1, a, d]))
    for copy in wloads:
        copy.start()

    barrier = pltpu.get_barrier_semaphore()

    def greet(dev):
        pl.semaphore_signal(barrier, inc=1, device_id={"slab": dev}, device_id_type=MESH)

    for k in range(1, cols):
        greet(peer(k))
    for cond, dev in ((has_before, me - 1), (has_after, me + 1), (has_lo, zlo), (has_hi, zhi)):
        @pl.when(cond)
        def _(dev=dev):
            greet(dev)
    partners = cols - 1
    for cond in (has_before, has_after, has_lo, has_hi):
        partners = partners + cond.astype(jnp.int32)
    pl.semaphore_wait(barrier, partners)

    def remote(src, dst, ssem, rsem, dev):
        return pltpu.make_async_remote_copy(
            src_ref=src, dst_ref=dst, send_sem=ssem, recv_sem=rsem,
            device_id={"slab": dev}, device_id_type=MESH)

    def halo(which, src, dst, up):
        if up:
            return remote(src.at[1], dst.at[0, inner], s_hs.at[which, 0], s_hr.at[which, 0], me + 1)
        return remote(src.at[0], dst.at[3, inner], s_hs.at[which, 1], s_hr.at[which, 1], me - 1)

    for which, src, dst in ((0, vol, vp), (1, grd, gp)):
        @pl.when(has_after)
        def _(which=which, src=src, dst=dst):
            halo(which, src, dst, True).start()

        @pl.when(has_before)
        def _(which=which, src=src, dst=dst):
            halo(which, src, dst, False).start()

    edge = jnp.zeros((breadth, ch), BF16)
    for ref in (vp, gp):
        for p in range(4):
            ref[p, pl.ds(0, breadth), :] = edge
            ref[p, pl.ds(breadth + cells, breadth), :] = edge
    edge2 = jnp.zeros((breadth, 2 * ch), BF16)
    for c in range(3):
        gs[c, pl.ds(0, breadth), :] = edge2
        gs[c, pl.ds(breadth + cells, breadth), :] = edge2
    blank = jnp.zeros((3, 3, ch, ch), BF16)
    wf[:, :, pl.ds(0, ch), pl.ds(ch, ch)] = blank
    wf[:, :, pl.ds(3 * ch, ch), pl.ds(0, ch)] = blank
    wb[:, :, pl.ds(0, ch), pl.ds(3 * ch, ch)] = blank
    wb[:, :, pl.ds(ch, ch), pl.ds(0, ch)] = blank
    for cond, p in ((me == 0, 0), (me == n - 1, 3)):
        @pl.when(cond)
        def _(p=p):
            vp[p, inner, :] = jnp.zeros((cells, ch), BF16)
            gp[p, inner, :] = jnp.zeros((cells, ch), BF16)

    rows = tile * breadth
    tiles = height // tile
    column = lax.rem(lax.broadcasted_iota(jnp.int32, (rows, 2 * ch), 0), breadth)

    def before_of(v):
        return jnp.where(column == 0, 0.0, pltpu.roll(v, 1, 0))

    def after_of(v):
        return jnp.where(column == breadth - 1, 0.0, pltpu.roll(v, rows - 1, 0))

    for copy in loads:
        copy.wait()

    def shift_tile(k, carry):
        at = pl.ds(pl.multiple_of(breadth + k * rows, 16), rows)
        both = jnp.concatenate([gp[1, at, :], gp[2, at, :]], axis=1)
        wide = both.astype(F32)
        gs[0, at, :] = after_of(wide).astype(BF16)
        gs[1, at, :] = both
        gs[2, at, :] = before_of(wide).astype(BF16)
        return carry

    lax.fori_loop(0, tiles, shift_tile, 0)

    def transpose_planes(lo, hi, at_row):
        def one(j, carry):
            at = pl.ds(pl.multiple_of(breadth + j * ch, 16), ch)
            to = pl.ds(pl.multiple_of(j * ch, ch), ch)
            xt[pl.ds(at_row, ch), to] = vp[lo, at, :].T
            xt[pl.ds(at_row + ch, ch), to] = vp[hi, at, :].T
            return carry
        lax.fori_loop(0, cells // ch, one, 0)

    def products(t, at_row):
        b, c = t // 3, lax.rem(t, 3)
        at = pl.ds(pl.multiple_of((2 - b) * breadth, 16), cells)
        return jnp.dot(xt[pl.ds(at_row, 2 * ch), :], gs[c, at, :], preferred_element_type=F32)

    transpose_planes(1, 2, 0)

    def own_part(t, carry):
        full = products(t, 0)
        acc[0, t] = full[:ch, ch:]
        acc[1, t] = full[:ch, :ch] + full[ch:, ch:]
        acc[2, t] = full[ch:, :ch]
        return carry

    lax.fori_loop(0, taps, own_part, 0)

    def halo_wait(which, src, dst):
        @pl.when(has_before)
        def _():
            halo(which, src, dst, True).wait_recv()

        @pl.when(has_after)
        def _():
            halo(which, src, dst, False).wait_recv()

    halo_wait(0, vol, vp)
    transpose_planes(0, 3, 2 * ch)

    mine = pl.ds(pl.multiple_of(core * half, half), half)
    other = pl.ds(pl.multiple_of((1 - core) * half, half), half)

    def root(j):
        return (line - 1) // 2 + lax.rem(j, 2) * (line // 2 - (line - 1) // 2)

    def to_sibling(j):
        return remote(acc.at[:, j, other], r_sib.at[j], s_sib.at[j], r_sibs.at[j], sib)

    def line_up(j):
        return remote(acc.at[:, j, mine], r_lo.at[j], s_line.at[j], r_los.at[j], zhi)

    def line_down(j):
        return remote(acc.at[:, j, mine], r_hi.at[j], s_line.at[j], r_his.at[j], zlo)

    def across(j, k):
        return remote(acc.at[:, j, mine], r_y.at[k - 1, j], s_y.at[k - 1, j], r_ys.at[k - 1, j], peer(k))

    def final_up(j):
        return remote(fin.at[:, j, mine], fin.at[:, j, mine], s_up.at[j], r_fin.at[j], zhi)

    def final_down(j):
        return remote(fin.at[:, j, mine], fin.at[:, j, mine], s_dn.at[j], r_fin.at[j], zlo)

    def final_sibling(j):
        return remote(fin.at[:, j, mine], fin.at[:, j, mine], s_fs.at[j], r_fsib.at[j], sib)

    def stage_send(j):
        full = products(j, 2 * ch)
        acc[0, j] = acc[0, j] + full[:ch, :ch]
        acc[2, j] = acc[2, j] + full[ch:, ch:]
        to_sibling(j).start()

    def stage_sibling(j):
        to_sibling(j).wait_recv()
        acc[:, j, mine, :] = acc[:, j, mine, :] + r_sib[j]

        @pl.when(jnp.logical_and(z == 0, root(j) != 0))
        def _():
            line_up(j).start()

        @pl.when(jnp.logical_and(z == line - 1, root(j) != line - 1))
        def _():
            line_down(j).start()

    def stage_line(j):
        @pl.when(jnp.logical_and(z > 0, z < root(j)))
        def _():
            line_up(j).wait_recv()
            acc[:, j, mine, :] = acc[:, j, mine, :] + r_lo[j]
            line_up(j).start()

        @pl.when(jnp.logical_and(z < line - 1, z > root(j)))
        def _():
            line_down(j).wait_recv()
            acc[:, j, mine, :] = acc[:, j, mine, :] + r_hi[j]
            line_down(j).start()

    def stage_root(j):
        @pl.when(z == root(j))
        def _():
            @pl.when(has_lo)
            def _():
                line_up(j).wait_recv()
                acc[:, j, mine, :] = acc[:, j, mine, :] + r_lo[j]

            @pl.when(has_hi)
            def _():
                line_down(j).wait_recv()
                acc[:, j, mine, :] = acc[:, j, mine, :] + r_hi[j]

            for k in range(1, cols):
                across(j, k).start()

    def stage_across(j):
        @pl.when(z == root(j))
        def _():
            for k in range(1, cols):
                across(j, k).wait_recv()
            if cols <= 2:
                total = acc[:, j, mine, :]
                for k in range(1, cols):
                    total = total + r_y[k - 1, j]
            else:
                total = jnp.zeros((3, half, ch), F32)
                for i in range(cols):
                    term = acc[:, j, mine, :]
                    for k in range(1, cols):
                        term = jnp.where(lax.rem(y + cols - k, cols) == i, r_y[k - 1, j], term)
                    total = total + term
            fin[:, j, mine, :] = total * factor

            @pl.when(has_lo)
            def _():
                final_down(j).start()

            @pl.when(has_hi)
            def _():
                final_up(j).start()

            final_sibling(j).start()

    def stage_spread(j):
        @pl.when(z < root(j))
        def _():
            final_down(j).wait_recv()

            @pl.when(has_lo)
            def _():
                final_down(j).start()

            final_sibling(j).start()

        @pl.when(z > root(j))
        def _():
            final_up(j).wait_recv()

            @pl.when(has_hi)
            def _():
                final_up(j).start()

            final_sibling(j).start()

    def conv_tile(planes, weights, out, k, backward):
        start = k * rows
        bands = []
        for b in range(3):
            at = pl.ds(pl.multiple_of(start + b * breadth, 16), rows)
            for p in range(4):
                bands.append(planes[p, at, :])
        lhs = jnp.concatenate(bands, axis=1)
        sums = []
        for c in range(3):
            if backward:
                rhs = jnp.concatenate([weights[2 - b, 2 - c] for b in range(3)], axis=1)
                sums.append(lax.dot_general(
                    lhs, rhs, (((1,), (1,)), ((), ())), preferred_element_type=F32))
            else:
                rhs = jnp.concatenate([weights[b, c] for b in range(3)], axis=0)
                sums.append(jnp.dot(lhs, rhs, preferred_element_type=F32))
        total = (sums[1] + before_of(sums[0]) + after_of(sums[2])).astype(BF16)
        at = pl.ds(pl.multiple_of(start, 16), rows)
        out[0, at, :] = total[:, :ch]
        out[1, at, :] = total[:, ch:]

    for copy in wloads:
        copy.wait()

    def during(j, stage):
        @pl.when(jnp.logical_and(j >= 0, j < taps))
        def _():
            stage(j)

    lags = (
        (6, stage_spread), (4, stage_across), (3, stage_root),
        (2, stage_line), (1, stage_sibling), (0, stage_send),
    )
    steps = max(taps + 6, 2 * tiles)

    def step(s, carry):
        for lag, stage in lags:
            during(s - lag, stage)

        @pl.when(s < tiles)
        def _():
            conv_tile(vp, wf, act, s, False)

        @pl.when(s == tiles)
        def _():
            halo_wait(1, grd, gp)

        @pl.when(jnp.logical_and(s >= tiles, s < 2 * tiles))
        def _():
            conv_tile(gp, wb, ing, s - tiles, True)
        return carry

    lax.fori_loop(0, steps, step, 0)

    act_copy = pltpu.make_async_copy(act, act_out, s_out.at[0])
    ing_copy = pltpu.make_async_copy(ing, ing_out, s_out.at[1])
    dw_copy = pltpu.make_async_copy(fin, dw_out, s_out.at[2])
    act_copy.start()
    ing_copy.start()

    def finish(j, carry):
        to_sibling(j).wait_send()
        final_sibling(j).wait_send()

        @pl.when(z != root(j))
        def _():
            line_up(j).wait_send()

        @pl.when(z == root(j))
        def _():
            for k in range(1, cols):
                across(j, k).wait_send()

        @pl.when(jnp.logical_and(has_lo, z <= root(j)))
        def _():
            final_down(j).wait_send()

        @pl.when(jnp.logical_and(has_hi, z >= root(j)))
        def _():
            final_up(j).wait_send()

        final_sibling(j).wait_recv()
        return carry

    lax.fori_loop(0, taps, finish, 0)
    dw_copy.start()

    for which, src, dst in ((0, vol, vp), (1, grd, gp)):
        @pl.when(has_after)
        def _(which=which, src=src, dst=dst):
            halo(which, src, dst, True).wait_send()

        @pl.when(has_before)
        def _(which=which, src=src, dst=dst):
            halo(which, src, dst, False).wait_send()

    act_copy.wait()
    ing_copy.wait()
    dw_copy.wait()


def body(n, line, cols, volume, kernel, grad_out):
    planes, height, breadth, ch = volume.shape
    cells = height * breadth
    half = ch // 2
    taps = 9
    tile = 8
    factor = float(np.float32(1.0) / np.sqrt(np.float32(n * planes * cells)))
    dma = pltpu.SemaphoreType.DMA
    peers = max(cols - 1, 1)
    flops = 3 * 2 * 27 * planes * cells * ch * ch
    outs = pl.pallas_call(
        functools.partial(layer_kernel, n, line, cols, height, breadth, ch, tile, factor),
        out_shape=(
            jax.ShapeDtypeStruct((planes, cells, ch), BF16),
            jax.ShapeDtypeStruct((planes, cells, ch), BF16),
            jax.ShapeDtypeStruct((3, taps, ch, ch), F32),
        ),
        in_specs=[pl.BlockSpec(memory_space=pl.ANY)] * 3,
        out_specs=[pl.BlockSpec(memory_space=pl.ANY)] * 3,
        scratch_shapes=[
            pltpu.VMEM((4, cells + 2 * breadth, ch), BF16),
            pltpu.VMEM((4, cells + 2 * breadth, ch), BF16),
            pltpu.VMEM((3, 3, 4 * ch, 2 * ch), BF16),
            pltpu.VMEM((3, 3, 2 * ch, 4 * ch), BF16),
            pltpu.VMEM((4 * ch, cells), BF16),
            pltpu.VMEM((3, cells + 2 * breadth, 2 * ch), BF16),
            pltpu.VMEM((3, taps, ch, ch), F32),
            pltpu.VMEM((3, taps, ch, ch), F32),
            pltpu.VMEM((taps, 3, half, ch), F32),
            pltpu.VMEM((taps, 3, half, ch), F32),
            pltpu.VMEM((taps, 3, half, ch), F32),
            pltpu.VMEM((peers, taps, 3, half, ch), F32),
            pltpu.VMEM((planes, cells, ch), BF16),
            pltpu.VMEM((planes, cells, ch), BF16),
            dma((4,)), dma((2, 3, 2)), dma((2, 2)), dma((2, 2)),
            dma((taps,)), dma((taps,)), dma((taps,)), dma((taps,)), dma((taps,)),
            dma((peers, taps)), dma((peers, taps)),
            dma((taps,)), dma((taps,)), dma((taps,)), dma((taps,)), dma((taps,)),
            dma((3,)),
        ],
        compiler_params=pltpu.CompilerParams(
            collective_id=0, has_side_effects=True, vmem_limit_bytes=56 * 1024 * 1024),
        cost_estimate=pl.CostEstimate(flops=flops, bytes_accessed=10_000_000, transcendentals=0),
    )(
        volume.reshape(planes, cells, ch),
        kernel,
        grad_out.reshape(planes, cells, ch),
    )
    activation = outs[0].reshape(volume.shape)
    input_grad = outs[1].reshape(volume.shape)
    return activation, input_grad, outs[2].reshape(3, 3, 3, ch, ch)


def solution(mesh):
    n = mesh.shape["slab"]
    chips = n // 2
    cols = 1
    while cols * cols * 4 <= chips:
        cols *= 2
    line = chips // cols
    return jax.shard_map(
        functools.partial(body, n, line, cols),
        mesh=mesh,
        in_specs=(
            P(("groups", "slab"), None, None, None),
            P(),
            P(("groups", "slab"), None, None, None),
        ),
        out_specs=(
            P(("groups", "slab"), None, None, None),
            P(("groups", "slab"), None, None, None),
            P("groups", None, None, None, None),
        ),
        check_vma=False,
    )
```

profile of v0, /device:TPU:0, one launch (start us, length us, event | category | flops | bytes accessed | tf_op | source)
XLA Modules:
  0.0 85.9 jit_solution(14440369049455426762)
XLA Ops:
  0.6 79.7 %shard_map.58 = (bf16[2,2304,128]{2,1,0:T(8,128)(2,1)}, bf16[2,2304,128]{2,1,0:T(8,128)(2,1)}, f32[3,9,128,128]{3,2,1,0:T(8,128)}) custom-call(bf16[2,2304,128]{2,1,0:T(8,128)(2,1)} %bitcast.8, bf16[3,3,3,128,128]{4,3,2,1,0:T(8,128)(2,1)} %ker.1, bf16[2,2304,128]{2,1,0:T(8,128)(2,1)} %bitcast.9), custom_call_target="tpu_custom_call" | custom-call | flops 12230590464 | bytes 10000000 | tf_op jit(solution)/shard_map/pallas_call | solution.py:412
  80.4 0.0 copy-start.1
  80.4 2.5 %copy.9 = bf16[2,48,48,128]{3,2,1,0:T(8,128)(2,1)} copy(bf16[2,48,48,128]{3,2,1,0:T(8,128)(2,1)} %bitcast.7) | data formatting | bytes 2359296
  82.8 0.0 copy-done.1
  82.8 0.0 copy-start
  82.8 1.0 %copy.10 = bf16[2,48,48,128]{3,2,1,0:T(8,128)(2,1)} copy(bf16[2,48,48,128]{3,2,1,0:T(8,128)(2,1)S(1)} %bitcast.6) | data formatting | bytes 2359296
  83.8 0.9 %copy-done = f32[3,9,128,128]{3,2,1,0:T(8,128)S(1)} copy-done((f32[3,9,128,128]{3,2,1,0:T(8,128)S(1)}, f32[3,9,128,128]{3,2,1,0:T(8,128)}, u32[]{:S(2)}) %copy-start) | copy-done | bytes 1769496
  84.7 1.2 %copy.11 = f32[3,3,3,128,128]{4,3,2,1,0:T(8,128)} copy(f32[3,3,3,128,128]{4,3,2,1,0:T(8,128)S(1)} %bitcast.5) | data formatting | bytes 3538944
Async XLA Ops:
  80.4 2.5 %copy-start.1 = (bf16[2,2304,128]{2,1,0:T(8,128)(2,1)S(1)}, bf16[2,2304,128]{2,1,0:T(8,128)(2,1)}, u32[]{:S(2)}) copy-start(bf16[2,2304,128]{2,1,0:T(8,128)(2,1)} %get-tuple-element.7) | copy-start | bytes 3538948
  82.8 1.9 %copy-start = (f32[3,9,128,128]{3,2,1,0:T(8,128)S(1)}, f32[3,9,128,128]{3,2,1,0:T(8,128)}, u32[]{:S(2)}) copy-start(f32[3,9,128,128]{3,2,1,0:T(8,128)} %get-tuple-element.8) | copy-start | bytes 5308420
where the time goes:
time: 86.2 us; the launch traced here: 85.9 us
  Pallas kernels  79.7 us (92%)
  local copies, waits for them, and re-layouts  5.57 us (6%)
    pallas_call x1, Pallas kernels, body(): pl.pallas_call(functools.partial(layer_kernel, n, line, cols, height, bre...  79.7 us
    unnamed x7, local copies, waits for them, and re-layouts  5.57 us

commit v1 on v0

--- a/solution.py
+++ b/solution.py
@@ -47,14 +47,13 @@
     for copy in loads:
         copy.start()
     wloads = []
+    for c in range(3):
+        wloads.append(pltpu.make_async_copy(
+            ker.at[:, :, c], wf.at[:, :, :, pl.ds(c * ch, ch)], s_w.at[0, c]))
     for a in range(3):
-        for d in range(2):
-            p = a + d
+        for b in range(3):
             wloads.append(pltpu.make_async_copy(
-                ker.at[a], wf.at[:, :, pl.ds(p * ch, ch), pl.ds(d * ch, ch)], s_w.at[0, a, d]))
-            p = d + 2 - a
-            wloads.append(pltpu.make_async_copy(
-                ker.at[a], wb.at[:, :, pl.ds(d * ch, ch), pl.ds(p * ch, ch)], s_w.at[1, a, d]))
+                ker.at[a, b], wb.at[:, :, pl.ds((8 - 3 * a - b) * ch, ch)], s_w.at[1 + a, b]))
     for copy in wloads:
         copy.start()
 
@@ -79,34 +78,41 @@
             src_ref=src, dst_ref=dst, send_sem=ssem, recv_sem=rsem,
             device_id={"slab": dev}, device_id_type=MESH)
 
-    def halo(which, src, dst, up):
-        if up:
-            return remote(src.at[1], dst.at[0, inner], s_hs.at[which, 0], s_hr.at[which, 0], me + 1)
-        return remote(src.at[0], dst.at[3, inner], s_hs.at[which, 1], s_hr.at[which, 1], me - 1)
-
-    for which, src, dst in ((0, vol, vp), (1, grd, gp)):
-        @pl.when(has_after)
-        def _(which=which, src=src, dst=dst):
-            halo(which, src, dst, True).start()
-
-        @pl.when(has_before)
-        def _(which=which, src=src, dst=dst):
-            halo(which, src, dst, False).start()
+    off_chip = jnp.where(core == 0, has_before, has_after)
+    off_dev = me - 1 + 2 * core
+    inside = 1 - core
+    slot_sib, slot_off = 3 * inside, 3 * core
+
+    def halo_sibling(which, src, dst):
+        return remote(src.at[inside], dst.at[3 * core, inner], s_hs.at[which, 0], s_hr.at[which, 0], sib)
+
+    def halo_off(which, src, dst):
+        return remote(src.at[core], dst.at[3 * inside, inner], s_hs.at[which, 1], s_hr.at[which, 1], off_dev)
+
+    def await_sibling(which, src, dst):
+        remote(src.at[inside], dst.at[slot_sib, inner], s_hs.at[which, 0], s_hr.at[which, 0], sib).wait_recv()
+
+    def await_off(which, src, dst):
+        @pl.when(off_chip)
+        def _():
+            remote(src.at[core], dst.at[slot_off, inner], s_hs.at[which, 1], s_hr.at[which, 1], off_dev).wait_recv()
+
+    @pl.when(off_chip)
+    def _():
+        halo_off(0, vol, vp).start()
+
+    halo_sibling(0, vol, vp).start()
+    halo_sibling(1, grd, gp).start()
 
     edge = jnp.zeros((breadth, ch), BF16)
     for ref in (vp, gp):
         for p in range(4):
             ref[p, pl.ds(0, breadth), :] = edge
             ref[p, pl.ds(breadth + cells, breadth), :] = edge
-    edge2 = jnp.zeros((breadth, 2 * ch), BF16)
     for c in range(3):
-        gs[c, pl.ds(0, breadth), :] = edge2
-        gs[c, pl.ds(breadth + cells, breadth), :] = edge2
-    blank = jnp.zeros((3, 3, ch, ch), BF16)
-    wf[:, :, pl.ds(0, ch), pl.ds(ch, ch)] = blank
-    wf[:, :, pl.ds(3 * ch, ch), pl.ds(0, ch)] = blank
-    wb[:, :, pl.ds(0, ch), pl.ds(3 * ch, ch)] = blank
-    wb[:, :, pl.ds(ch, ch), pl.ds(0, ch)] = blank
+        for d in range(2):
+            gs[c, d, pl.ds(0, breadth), :] = edge
+            gs[c, d, pl.ds(breadth + cells, breadth), :] = edge
     for cond, p in ((me == 0, 0), (me == n - 1, 3)):
         @pl.when(cond)
         def _(p=p):
@@ -115,7 +121,7 @@
 
     rows = tile * breadth
     tiles = height // tile
-    column = lax.rem(lax.broadcasted_iota(jnp.int32, (rows, 2 * ch), 0), breadth)
+    column = lax.rem(lax.broadcasted_iota(jnp.int32, (rows, ch), 0), breadth)
 
     def before_of(v):
         return jnp.where(column == 0, 0.0, pltpu.roll(v, 1, 0))
@@ -128,51 +134,84 @@
 
     def shift_tile(k, carry):
         at = pl.ds(pl.multiple_of(breadth + k * rows, 16), rows)
-        both = jnp.concatenate([gp[1, at, :], gp[2, at, :]], axis=1)
-        wide = both.astype(F32)
-        gs[0, at, :] = after_of(wide).astype(BF16)
-        gs[1, at, :] = both
-        gs[2, at, :] = before_of(wide).astype(BF16)
+        for d in range(2):
+            plane = gp[d + 1, at, :]
+            wide = plane.astype(F32)
+            gs[0, d, at, :] = after_of(wide).astype(BF16)
+            gs[1, d, at, :] = plane
+            gs[2, d, at, :] = before_of(wide).astype(BF16)
         return carry
 
     lax.fori_loop(0, tiles, shift_tile, 0)
 
-    def transpose_planes(lo, hi, at_row):
+    def transpose_planes(pairs):
         def one(j, carry):
             at = pl.ds(pl.multiple_of(breadth + j * ch, 16), ch)
             to = pl.ds(pl.multiple_of(j * ch, ch), ch)
-            xt[pl.ds(at_row, ch), to] = vp[lo, at, :].T
-            xt[pl.ds(at_row + ch, ch), to] = vp[hi, at, :].T
+            for p, row in pairs:
+                xt[pl.ds(row * ch, ch), to] = vp[p, at, :].T
             return carry
         lax.fori_loop(0, cells // ch, one, 0)
 
-    def products(t, at_row):
+    def grads(t, d):
         b, c = t // 3, lax.rem(t, 3)
-        at = pl.ds(pl.multiple_of((2 - b) * breadth, 16), cells)
-        return jnp.dot(xt[pl.ds(at_row, 2 * ch), :], gs[c, at, :], preferred_element_type=F32)
-
-    transpose_planes(1, 2, 0)
+        return gs[c, d, pl.ds(pl.multiple_of((2 - b) * breadth, 16), cells), :]
+
+    await_sibling(0, vol, vp)
+    transpose_planes(((1, 0), (2, 1), (slot_sib, 2)))
 
     def own_part(t, carry):
-        full = products(t, 0)
-        acc[0, t] = full[:ch, ch:]
-        acc[1, t] = full[:ch, :ch] + full[ch:, ch:]
-        acc[2, t] = full[ch:, :ch]
+        rhs = jnp.concatenate([grads(t, 0), grads(t, 1)], axis=1)
+        full = jnp.dot(xt[pl.ds(0, 3 * ch), :], rhs, preferred_element_type=F32)
+        beside = full[2 * ch:]
+        acc[0, t] = full[:ch, ch:] + jnp.where(core == 1, beside[:, :ch], 0.0)
+        acc[1, t] = full[:ch, :ch] + full[ch:2 * ch, ch:]
+        acc[2, t] = full[ch:2 * ch, :ch] + jnp.where(core == 0, beside[:, ch:], 0.0)
         return carry
 
     lax.fori_loop(0, taps, own_part, 0)
 
-    def halo_wait(which, src, dst):
-        @pl.when(has_before)
-        def _():
-            halo(which, src, dst, True).wait_recv()
-
-        @pl.when(has_after)
-        def _():
-            halo(which, src, dst, False).wait_recv()
-
-    halo_wait(0, vol, vp)
-    transpose_planes(0, 3, 2 * ch)
+    def conv_tile(planes, weights, out, d, k, backward):
+        start = k * rows
+        bands = []
+        for a in range(3):
+            for b in range(3):
+                at = pl.ds(pl.multiple_of(start + b * breadth, 16), rows)
+                bands.append(planes[d + a, at, :])
+        lhs = jnp.concatenate(bands, axis=1)
+        if backward:
+            rhs = jnp.concatenate([weights[c] for c in range(3)], axis=0)
+            sums = lax.dot_general(lhs, rhs, (((1,), (1,)), ((), ())), preferred_element_type=F32)
+            first, last = sums[:, 2 * ch:], sums[:, :ch]
+        else:
+            rhs = jnp.concatenate([weights[a, b] for a in range(3) for b in range(3)], axis=0)
+            sums = jnp.dot(lhs, rhs, preferred_element_type=F32)
+            first, last = sums[:, :ch], sums[:, 2 * ch:]
+        total = sums[:, ch:2 * ch] + before_of(first) + after_of(last)
+        out[d, pl.ds(pl.multiple_of(start, 16), rows), :] = total.astype(BF16)
+
+    for copy in wloads:
+        copy.wait()
+
+    def inside_act(k, carry):
+        conv_tile(vp, wf, act, inside, k, False)
+        return carry
+
+    def inside_ing(k, carry):
+        conv_tile(gp, wb, ing, inside, k, True)
+        return carry
+
+    lax.fori_loop(0, tiles, inside_act, 0)
+    await_sibling(1, grd, gp)
+    lax.fori_loop(0, tiles, inside_ing, 0)
+
+    await_off(0, vol, vp)
+
+    @pl.when(off_chip)
+    def _():
+        halo_off(1, grd, gp).start()
+
+    transpose_planes(((slot_off, 3),))
 
     mine = pl.ds(pl.multiple_of(core * half, half), half)
     other = pl.ds(pl.multiple_of((1 - core) * half, half), half)
@@ -202,9 +241,8 @@
         return remote(fin.at[:, j, mine], fin.at[:, j, mine], s_fs.at[j], r_fsib.at[j], sib)
 
     def stage_send(j):
-        full = products(j, 2 * ch)
-        acc[0, j] = acc[0, j] + full[:ch, :ch]
-        acc[2, j] = acc[2, j] + full[ch:, ch:]
+        part = jnp.dot(xt[pl.ds(3 * ch, ch), :], grads(j, core), preferred_element_type=F32)
+        acc[2 * core, j] = acc[2 * core, j] + part
         to_sibling(j).start()
 
     def stage_sibling(j):
@@ -297,31 +335,6 @@
 
             final_sibling(j).start()
 
-    def conv_tile(planes, weights, out, k, backward):
-        start = k * rows
-        bands = []
-        for b in range(3):
-            at = pl.ds(pl.multiple_of(start + b * breadth, 16), rows)
-            for p in range(4):
-                bands.append(planes[p, at, :])
-        lhs = jnp.concatenate(bands, axis=1)
-        sums = []
-        for c in range(3):
-            if backward:
-                rhs = jnp.concatenate([weights[2 - b, 2 - c] for b in range(3)], axis=1)
-                sums.append(lax.dot_general(
-                    lhs, rhs, (((1,), (1,)), ((), ())), preferred_element_type=F32))
-            else:
-                rhs = jnp.concatenate([weights[b, c] for b in range(3)], axis=0)
-                sums.append(jnp.dot(lhs, rhs, preferred_element_type=F32))
-        total = (sums[1] + before_of(sums[0]) + after_of(sums[2])).astype(BF16)
-        at = pl.ds(pl.multiple_of(start, 16), rows)
-        out[0, at, :] = total[:, :ch]
-        out[1, at, :] = total[:, ch:]
-
-    for copy in wloads:
-        copy.wait()
-
     def during(j, stage):
         @pl.when(jnp.logical_and(j >= 0, j < taps))
         def _():
@@ -339,15 +352,15 @@
 
         @pl.when(s < tiles)
         def _():
-            conv_tile(vp, wf, act, s, False)
+            conv_tile(vp, wf, act, core, s, False)
 
         @pl.when(s == tiles)
         def _():
-            halo_wait(1, grd, gp)
+            await_off(1, grd, gp)
 
         @pl.when(jnp.logical_and(s >= tiles, s < 2 * tiles))
         def _():
-            conv_tile(gp, wb, ing, s - tiles, True)
+            conv_tile(gp, wb, ing, core, s - tiles, True)
         return carry
 
     lax.fori_loop(0, steps, step, 0)
@@ -386,13 +399,11 @@
     dw_copy.start()
 
     for which, src, dst in ((0, vol, vp), (1, grd, gp)):
-        @pl.when(has_after)
+        halo_sibling(which, src, dst).wait_send()
+
+        @pl.when(off_chip)
         def _(which=which, src=src, dst=dst):
-            halo(which, src, dst, True).wait_send()
-
-        @pl.when(has_before)
-        def _(which=which, src=src, dst=dst):
-            halo(which, src, dst, False).wait_send()
+            halo_off(which, src, dst).wait_send()
 
     act_copy.wait()
     ing_copy.wait()
@@ -421,10 +432,10 @@
         scratch_shapes=[
             pltpu.VMEM((4, cells + 2 * breadth, ch), BF16),
             pltpu.VMEM((4, cells + 2 * breadth, ch), BF16),
-            pltpu.VMEM((3, 3, 4 * ch, 2 * ch), BF16),
-            pltpu.VMEM((3, 3, 2 * ch, 4 * ch), BF16),
+            pltpu.VMEM((3, 3, ch, 3 * ch), BF16),
+            pltpu.VMEM((3, ch, 9 * ch), BF16),
             pltpu.VMEM((4 * ch, cells), BF16),
-            pltpu.VMEM((3, cells + 2 * breadth, 2 * ch), BF16),
+            pltpu.VMEM((3, 2, cells + 2 * breadth, ch), BF16),
             pltpu.VMEM((3, taps, ch, ch), F32),
             pltpu.VMEM((3, taps, ch, ch), F32),
             pltpu.VMEM((taps, 3, half, ch), F32),
@@ -433,7 +444,7 @@
             pltpu.VMEM((peers, taps, 3, half, ch), F32),
             pltpu.VMEM((planes, cells, ch), BF16),
             pltpu.VMEM((planes, cells, ch), BF16),
-            dma((4,)), dma((2, 3, 2)), dma((2, 2)), dma((2, 2)),
+            dma((4,)), dma((4, 3)), dma((2, 2)), dma((2, 2)),
             dma((taps,)), dma((taps,)), dma((taps,)), dma((taps,)), dma((taps,)),
             dma((peers, taps)), dma((peers, taps)),
             dma((taps,)), dma((taps,)), dma((taps,)), dma((taps,)), dma((taps,)),

time: 86.2 us -> 89.4 us (1.037)
  Pallas kernels: 79.7 us -> 83 us
    pallas_call x1, Pallas kernels: 79.7 us -> 83 us  [body(): pl.pallas_call(functools.partial(layer_kernel, n, line, cols, height, bre...]
where the time goes in v1:
time: 89.4 us; the launch traced here: 89.2 us
  Pallas kernels  83 us (93%)
  local copies, waits for them, and re-layouts  5.57 us (6%)
    pallas_call x1, Pallas kernels, body(): pl.pallas_call(functools.partial(layer_kernel, n, line, cols, height, bre...  83 us
    unnamed x7, local copies, waits for them, and re-layouts  5.57 us

profile of v1, /device:TPU:0, one launch (start us, length us, event | category | flops | bytes accessed | tf_op | source)
XLA Modules:
  0.0 89.2 jit_solution(2380192089765258638)
XLA Ops:
  0.6 83.0 %shard_map.58 = (bf16[2,2304,128]{2,1,0:T(8,128)(2,1)}, bf16[2,2304,128]{2,1,0:T(8,128)(2,1)}, f32[3,9,128,128]{3,2,1,0:T(8,128)}) custom-call(bf16[2,2304,128]{2,1,0:T(8,128)(2,1)} %bitcast.8, bf16[3,3,3,128,128]{4,3,2,1,0:T(8,128)(2,1)} %ker.1, bf16[2,2304,128]{2,1,0:T(8,128)(2,1)} %bitcast.9), custom_call_target="tpu_custom_call" | custom-call | flops 12230590464 | bytes 10000000 | tf_op jit(solution)/shard_map/pallas_call | solution.py:423
  83.7 0.0 copy-start.1
  83.7 2.5 %copy.9 = bf16[2,48,48,128]{3,2,1,0:T(8,128)(2,1)} copy(bf16[2,48,48,128]{3,2,1,0:T(8,128)(2,1)} %bitcast.7) | data formatting | bytes 2359296
  86.1 0.0 copy-done.1
  86.1 0.0 copy-start
  86.1 1.0 %copy.10 = bf16[2,48,48,128]{3,2,1,0:T(8,128)(2,1)} copy(bf16[2,48,48,128]{3,2,1,0:T(8,128)(2,1)S(1)} %bitcast.6) | data formatting | bytes 2359296
  87.2 0.9 copy-done
  88.0 1.2 %copy.11 = f32[3,3,3,128,128]{4,3,2,1,0:T(8,128)} copy(f32[3,3,3,128,128]{4,3,2,1,0:T(8,128)S(1)} %bitcast.5) | data formatting | bytes 3538944
Async XLA Ops:
  83.7 2.5 %copy-start.1 = (bf16[2,2304,128]{2,1,0:T(8,128)(2,1)S(1)}, bf16[2,2304,128]{2,1,0:T(8,128)(2,1)}, u32[]{:S(2)}) copy-start(bf16[2,2304,128]{2,1,0:T(8,128)(2,1)} %get-tuple-element.7) | copy-start | bytes 3538948
  86.1 1.9 %copy-start = (f32[3,9,128,128]{3,2,1,0:T(8,128)S(1)}, f32[3,9,128,128]{3,2,1,0:T(8,128)}, u32[]{:S(2)}) copy-start(f32[3,9,128,128]{3,2,1,0:T(8,128)} %get-tuple-element.8) | copy-start | bytes 5308420

commit v2 on v1

--- a/solution.py
+++ b/solution.py
@@ -15,10 +15,10 @@
 
 def layer_kernel(
     n, line, cols, height, breadth, ch, tile, factor,
-    vol, ker, grd,
-    act_out, ing_out, dw_out,
-    vp, gp, wf, wb, xt, gs, acc, fin, r_sib, r_lo, r_hi, r_y, act, ing,
-    s_in, s_w, s_hs, s_hr, s_sib, r_sibs, s_line, r_los, r_his, s_y, r_ys,
+    vol, grd,
+    vh_out, gh_out, dw_out,
+    vp, gp, xt, gs, acc, fin, r_sib, r_lo, r_hi, r_y,
+    s_in, s_hs, s_hr, s_sib, r_sibs, s_line, r_los, r_his, s_y, r_ys,
     s_up, s_dn, s_fs, r_fin, r_fsib, s_out,
 ):
     cells = height * breadth
@@ -46,17 +46,6 @@
         loads.append(pltpu.make_async_copy(grd.at[p], gp.at[p + 1, inner], s_in.at[p + 2]))
     for copy in loads:
         copy.start()
-    wloads = []
-    for c in range(3):
-        wloads.append(pltpu.make_async_copy(
-            ker.at[:, :, c], wf.at[:, :, :, pl.ds(c * ch, ch)], s_w.at[0, c]))
-    for a in range(3):
-        for b in range(3):
-            wloads.append(pltpu.make_async_copy(
-                ker.at[a, b], wb.at[:, :, pl.ds((8 - 3 * a - b) * ch, ch)], s_w.at[1 + a, b]))
-    for copy in wloads:
-        copy.start()
-
     barrier = pltpu.get_barrier_semaphore()
 
     def greet(dev):
@@ -171,40 +160,7 @@
 
     lax.fori_loop(0, taps, own_part, 0)
 
-    def conv_tile(planes, weights, out, d, k, backward):
-        start = k * rows
-        bands = []
-        for a in range(3):
-            for b in range(3):
-                at = pl.ds(pl.multiple_of(start + b * breadth, 16), rows)
-                bands.append(planes[d + a, at, :])
-        lhs = jnp.concatenate(bands, axis=1)
-        if backward:
-            rhs = jnp.concatenate([weights[c] for c in range(3)], axis=0)
-            sums = lax.dot_general(lhs, rhs, (((1,), (1,)), ((), ())), preferred_element_type=F32)
-            first, last = sums[:, 2 * ch:], sums[:, :ch]
-        else:
-            rhs = jnp.concatenate([weights[a, b] for a in range(3) for b in range(3)], axis=0)
-            sums = jnp.dot(lhs, rhs, preferred_element_type=F32)
-            first, last = sums[:, :ch], sums[:, 2 * ch:]
-        total = sums[:, ch:2 * ch] + before_of(first) + after_of(last)
-        out[d, pl.ds(pl.multiple_of(start, 16), rows), :] = total.astype(BF16)
-
-    for copy in wloads:
-        copy.wait()
-
-    def inside_act(k, carry):
-        conv_tile(vp, wf, act, inside, k, False)
-        return carry
-
-    def inside_ing(k, carry):
-        conv_tile(gp, wb, ing, inside, k, True)
-        return carry
-
-    lax.fori_loop(0, tiles, inside_act, 0)
     await_sibling(1, grd, gp)
-    lax.fori_loop(0, tiles, inside_ing, 0)
-
     await_off(0, vol, vp)
 
     @pl.when(off_chip)
@@ -344,32 +300,24 @@
         (6, stage_spread), (4, stage_across), (3, stage_root),
         (2, stage_line), (1, stage_sibling), (0, stage_send),
     )
-    steps = max(taps + 6, 2 * tiles)
+    steps = taps + 6
 
     def step(s, carry):
         for lag, stage in lags:
             during(s - lag, stage)
 
-        @pl.when(s < tiles)
-        def _():
-            conv_tile(vp, wf, act, core, s, False)
-
-        @pl.when(s == tiles)
-        def _():
-            await_off(1, grd, gp)
-
-        @pl.when(jnp.logical_and(s >= tiles, s < 2 * tiles))
-        def _():
-            conv_tile(gp, wb, ing, core, s - tiles, True)
         return carry
 
     lax.fori_loop(0, steps, step, 0)
-
-    act_copy = pltpu.make_async_copy(act, act_out, s_out.at[0])
-    ing_copy = pltpu.make_async_copy(ing, ing_out, s_out.at[1])
-    dw_copy = pltpu.make_async_copy(fin, dw_out, s_out.at[2])
-    act_copy.start()
-    ing_copy.start()
+    await_off(1, grd, gp)
+
+    sides = []
+    for i, (planes, out) in enumerate(((vp, vh_out), (gp, gh_out))):
+        for k in range(2):
+            sides.append(pltpu.make_async_copy(planes.at[3 * k, inner], out.at[k], s_out.at[1 + 2 * i + k]))
+    for copy in sides:
+        copy.start()
+    dw_copy = pltpu.make_async_copy(fin, dw_out, s_out.at[0])
 
     def finish(j, carry):
         to_sibling(j).wait_send()
@@ -405,9 +353,86 @@
         def _(which=which, src=src, dst=dst):
             halo_off(which, src, dst).wait_send()
 
-    act_copy.wait()
-    ing_copy.wait()
+    for copy in sides:
+        copy.wait()
     dw_copy.wait()
+
+
+def load_planes(breadth, cells, ch, src, sides, planes, sem):
+    inner = pl.ds(breadth, cells)
+    copies = [pltpu.make_async_copy(src.at[k], planes.at[k + 1, inner], sem.at[k]) for k in range(2)]
+    copies += [pltpu.make_async_copy(sides.at[k], planes.at[3 * k, inner], sem.at[2 + k]) for k in range(2)]
+    for copy in copies:
+        copy.start()
+    edge = jnp.zeros((breadth, ch), BF16)
+    for p in range(4):
+        planes[p, pl.ds(0, breadth), :] = edge
+        planes[p, pl.ds(breadth + cells, breadth), :] = edge
+    return copies
+
+
+def shifted_sum(breadth, first, middle, last):
+    rows = first.shape[0]
+    column = lax.rem(lax.broadcasted_iota(jnp.int32, first.shape, 0), breadth)
+    before = jnp.where(column == 0, 0.0, pltpu.roll(first, 1, 0))
+    after = jnp.where(column == breadth - 1, 0.0, pltpu.roll(last, rows - 1, 0))
+    return (middle + before + after).astype(BF16)
+
+
+def conv_pair(height, breadth, ch, tile, src, sides, ker, out, planes, w, sem):
+    rows, tiles = tile * breadth, height // tile
+    copies = load_planes(breadth, height * breadth, ch, src, sides, planes, sem)
+    blank = jnp.zeros((3, 3, ch, ch), BF16)
+    for p in range(4):
+        for d in range(2):
+            value = ker[p - d] if 0 <= p - d <= 2 else blank
+            w[:, :, pl.ds(p * ch, ch), pl.ds(d * ch, ch)] = value
+    for copy in copies:
+        copy.wait()
+
+    def one(k, carry):
+        bands = []
+        for b in range(3):
+            at = pl.ds(pl.multiple_of(k * rows + b * breadth, 16), rows)
+            bands += [planes[p, at, :] for p in range(4)]
+        lhs = jnp.concatenate(bands, axis=1)
+        sums = [
+            jnp.dot(lhs, jnp.concatenate([w[b, c] for b in range(3)], axis=0), preferred_element_type=F32)
+            for c in range(3)
+        ]
+        total = shifted_sum(breadth, *sums)
+        at = pl.ds(pl.multiple_of(k * rows, 16), rows)
+        out[0, at, :] = total[:, :ch]
+        out[1, at, :] = total[:, ch:]
+        return carry
+
+    lax.fori_loop(0, tiles, one, 0)
+
+
+def conv_single(height, breadth, ch, tile, src, sides, ker, out, planes, w, sem):
+    rows, tiles = tile * breadth, height // tile
+    copies = load_planes(breadth, height * breadth, ch, src, sides, planes, sem)
+    for a in range(3):
+        for b in range(3):
+            for c in range(3):
+                w[pl.ds((3 * a + b) * ch, ch), pl.ds(c * ch, ch)] = ker[2 - a, 2 - b, 2 - c].T
+    for copy in copies:
+        copy.wait()
+
+    def one(i, carry):
+        d, k = i // tiles, lax.rem(i, tiles)
+        bands = []
+        for a in range(3):
+            for b in range(3):
+                at = pl.ds(pl.multiple_of(k * rows + b * breadth, 16), rows)
+                bands.append(planes[d + a, at, :])
+        lhs = jnp.concatenate(bands, axis=1)
+        sums = jnp.dot(lhs, w[...], preferred_element_type=F32)
+        total = shifted_sum(breadth, *(sums[:, c * ch:(c + 1) * ch] for c in range(3)))
+        out[d, pl.ds(pl.multiple_of(k * rows, 16), rows), :] = total
+        return carry
+
+    lax.fori_loop(0, 2 * tiles, one, 0)
 
 
 def body(n, line, cols, volume, kernel, grad_out):
@@ -420,20 +445,20 @@
     dma = pltpu.SemaphoreType.DMA
     peers = max(cols - 1, 1)
     flops = 3 * 2 * 27 * planes * cells * ch * ch
+    vol = volume.reshape(planes, cells, ch)
+    grd = grad_out.reshape(planes, cells, ch)
     outs = pl.pallas_call(
         functools.partial(layer_kernel, n, line, cols, height, breadth, ch, tile, factor),
         out_shape=(
-            jax.ShapeDtypeStruct((planes, cells, ch), BF16),
-            jax.ShapeDtypeStruct((planes, cells, ch), BF16),
+            jax.ShapeDtypeStruct((2, cells, ch), BF16),
+            jax.ShapeDtypeStruct((2, cells, ch), BF16),
             jax.ShapeDtypeStruct((3, taps, ch, ch), F32),
         ),
-        in_specs=[pl.BlockSpec(memory_space=pl.ANY)] * 3,
+        in_specs=[pl.BlockSpec(memory_space=pl.ANY)] * 2,
         out_specs=[pl.BlockSpec(memory_space=pl.ANY)] * 3,
         scratch_shapes=[
             pltpu.VMEM((4, cells + 2 * breadth, ch), BF16),
             pltpu.VMEM((4, cells + 2 * breadth, ch), BF16),
-            pltpu.VMEM((3, 3, ch, 3 * ch), BF16),
-            pltpu.VMEM((3, ch, 9 * ch), BF16),
             pltpu.VMEM((4 * ch, cells), BF16),
             pltpu.VMEM((3, 2, cells + 2 * breadth, ch), BF16),
             pltpu.VMEM((3, taps, ch, ch), F32),
@@ -442,25 +467,40 @@
             pltpu.VMEM((taps, 3, half, ch), F32),
             pltpu.VMEM((taps, 3, half, ch), F32),
             pltpu.VMEM((peers, taps, 3, half, ch), F32),
-            pltpu.VMEM((planes, cells, ch), BF16),
-            pltpu.VMEM((planes, cells, ch), BF16),
-            dma((4,)), dma((4, 3)), dma((2, 2)), dma((2, 2)),
+            dma((4,)), dma((2, 2)), dma((2, 2)),
             dma((taps,)), dma((taps,)), dma((taps,)), dma((taps,)), dma((taps,)),
             dma((peers, taps)), dma((peers, taps)),
             dma((taps,)), dma((taps,)), dma((taps,)), dma((taps,)), dma((taps,)),
-            dma((3,)),
+            dma((5,)),
         ],
         compiler_params=pltpu.CompilerParams(
             collective_id=0, has_side_effects=True, vmem_limit_bytes=56 * 1024 * 1024),
         cost_estimate=pl.CostEstimate(flops=flops, bytes_accessed=10_000_000, transcendentals=0),
-    )(
-        volume.reshape(planes, cells, ch),
-        kernel,
-        grad_out.reshape(planes, cells, ch),
+    )(vol, grd)
+    vmem = pl.BlockSpec(memory_space=pltpu.VMEM)
+    padded_rows = cells + 2 * breadth
+
+    def conv(kern, wshape):
+        return pl.pallas_call(
+            functools.partial(kern, height, breadth, ch, tile),
+            out_shape=jax.ShapeDtypeStruct((planes, cells, ch), BF16),
+            in_specs=[pl.BlockSpec(memory_space=pl.ANY), pl.BlockSpec(memory_space=pl.ANY), vmem],
+            out_specs=vmem,
+            scratch_shapes=[
+                pltpu.VMEM((4, padded_rows, ch), BF16),
+                pltpu.VMEM(wshape, BF16),
+                dma((4,)),
+            ],
+            compiler_params=pltpu.CompilerParams(vmem_limit_bytes=40 * 1024 * 1024),
+            cost_estimate=pl.CostEstimate(flops=flops // 3, bytes_accessed=5_000_000, transcendentals=0),
+        )
+
+    activation = conv(conv_pair, (3, 3, 4 * ch, 2 * ch))(vol, outs[0], kernel)
+    input_grad = conv(conv_single, (9 * ch, 3 * ch))(grd, outs[1], kernel)
+    return (
+        activation.reshape(volume.shape), input_grad.reshape(volume.shape),
+        outs[2].reshape(3, 3, 3, ch, ch),
     )
-    activation = outs[0].reshape(volume.shape)
-    input_grad = outs[1].reshape(volume.shape)
-    return activation, input_grad, outs[2].reshape(3, 3, 3, ch, ch)
 
 
 def solution(mesh):

time: 89.4 us -> 101 us (1.13)
  Pallas kernels: 83 us -> 97.1 us
  local copies, waits for them, and re-layouts: 5.57 us -> 2.49 us
    pallas_call x0 -> x2, Pallas kernels: none -> 18.2 us  [the longest x1 9.68 us: body(): input_grad = conv(conv_single, (9 * ch, 3 * ch))(grd, outs[1], kernel)]
    pallas_call x1, Pallas kernels: 83 us -> 78.9 us  [body(): pl.pallas_call(functools.partial(layer_kernel, n, line, cols, height, bre...]
    unnamed x7 -> x13, local copies, waits for them, and re-layouts: 5.57 us -> 2.49 us
where the time goes in v2:
time: 101 us; the launch traced here: 100 us
  Pallas kernels  97.1 us (96%)
  local copies, waits for them, and re-layouts  2.49 us (2%)
    pallas_call x1, Pallas kernels, body(): pl.pallas_call(functools.partial(layer_kernel, n, line, cols, height, bre...  78.9 us
    pallas_call x1, Pallas kernels, body(): input_grad = conv(conv_single, (9 * ch, 3 * ch))(grd, outs[1], kernel)  9.68 us
    pallas_call x1, Pallas kernels, body(): activation = conv(conv_pair, (3, 3, 4 * ch, 2 * ch))(vol, outs[0], kernel)  8.55 us
    unnamed x13, local copies, waits for them, and re-layouts  2.49 us

profile of v2, /device:TPU:0, one launch (start us, length us, event | category | flops | bytes accessed | tf_op | source)
XLA Modules:
  0.0 100.4 jit_solution(2268396822643843760)
XLA Ops:
  0.6 0.0 copy-start
  0.6 0.0 copy-start.2
  0.6 78.9 %shard_map.58 = (bf16[2,2304,128]{2,1,0:T(8,128)(2,1)}, bf16[2,2304,128]{2,1,0:T(8,128)(2,1)}, f32[3,9,128,128]{3,2,1,0:T(8,128)}) custom-call(bf16[2,2304,128]{2,1,0:T(8,128)(2,1)} %bitcast.5, bf16[2,2304,128]{2,1,0:T(8,128)(2,1)} %bitcast.7), custom_call_target="tpu_custom_call" | custom-call | flops 12230590464 | bytes 10000000 | tf_op jit(solution)/shard_map/pallas_call | solution.py:450
  79.6 0.0 copy-done
  79.6 0.0 copy-done.2
  79.6 0.0 copy-start.4
  79.6 1.3 %copy-done.4 = bf16[2,2304,128]{2,1,0:T(8,128)(2,1)S(1)} copy-done((bf16[2,2304,128]{2,1,0:T(8,128)(2,1)S(1)}, bf16[2,2304,128]{2,1,0:T(8,128)(2,1)}, u32[]{:S(2)}) %copy-start.4) | copy-done | bytes 1179672
  80.9 0.0 copy-start.1
  80.9 0.0 copy-start.3
  80.9 8.6 %shard_map.59 = bf16[2,2304,128]{2,1,0:T(8,128)(2,1)} custom-call(bf16[2,2304,128]{2,1,0:T(8,128)(2,1)S(1)} %bitcast.6, bf16[2,2304,128]{2,1,0:T(8,128)(2,1)S(1)} %copy-done.4, bf16[3,3,3,128,128]{4,3,2,1,0:T(8,128)(2,1)S(1)} %copy-done.2), custom_call_target="tpu_custom_call" | custom-call | flops 4076863488 | bytes 5000000 | tf_op jit(solution)/shard_map/pallas_call | solution.py:498
  89.4 0.0 copy-done.1
  89.4 0.0 copy-done.3
  89.4 0.0 copy-start.5
  89.4 9.7 %shard_map.60 = bf16[2,2304,128]{2,1,0:T(8,128)(2,1)} custom-call(bf16[2,2304,128]{2,1,0:T(8,128)(2,1)S(1)} %bitcast.8, bf16[2,2304,128]{2,1,0:T(8,128)(2,1)S(1)} %copy-done.3, bf16[3,3,3,128,128]{4,3,2,1,0:T(8,128)(2,1)S(1)} %copy-done.2), custom_call_target="tpu_custom_call" | custom-call | flops 4076863488 | bytes 5000000 | tf_op jit(solution)/shard_map/pallas_call | solution.py:499
  99.1 0.0 copy-done.5
  99.1 1.2 %copy.7 = f32[3,3,3,128,128]{4,3,2,1,0:T(8,128)} copy(f32[3,3,3,128,128]{4,3,2,1,0:T(8,128)S(1)} %bitcast.9) | data formatting | bytes 3538944
Async XLA Ops:
  0.6 78.9 %copy-start = (bf16[2,48,48,128]{3,2,1,0:T(8,128)(2,1)S(1)}, bf16[2,48,48,128]{3,2,1,0:T(8,128)(2,1)}, u32[]{:S(2)}) copy-start(bf16[2,48,48,128]{3,2,1,0:T(8,128)(2,1)} %param.3) | copy-start | bytes 3538948
  0.6 78.9 %copy-start.2 = (bf16[3,3,3,128,128]{4,3,2,1,0:T(8,128)(2,1)S(1)}, bf16[3,3,3,128,128]{4,3,2,1,0:T(8,128)(2,1)}, u32[]{:S(2)}) copy-start(bf16[3,3,3,128,128]{4,3,2,1,0:T(8,128)(2,1)} %ker.3) | copy-start | bytes 2654212
  79.6 1.3 %copy-start.4 = (bf16[2,2304,128]{2,1,0:T(8,128)(2,1)S(1)}, bf16[2,2304,128]{2,1,0:T(8,128)(2,1)}, u32[]{:S(2)}) copy-start(bf16[2,2304,128]{2,1,0:T(8,128)(2,1)} %get-tuple-element.6.sides) | copy-start | bytes 3538948
  80.9 8.6 %copy-start.1 = (bf16[2,48,48,128]{3,2,1,0:T(8,128)(2,1)S(1)}, bf16[2,48,48,128]{3,2,1,0:T(8,128)(2,1)}, u32[]{:S(2)}) copy-start(bf16[2,48,48,128]{3,2,1,0:T(8,128)(2,1)} %param.5) | copy-start | bytes 3538948
  80.9 8.6 %copy-start.3 = (bf16[2,2304,128]{2,1,0:T(8,128)(2,1)S(1)}, bf16[2,2304,128]{2,1,0:T(8,128)(2,1)}, u32[]{:S(2)}) copy-start(bf16[2,2304,128]{2,1,0:T(8,128)(2,1)} %get-tuple-element.7.sides) | copy-start | bytes 3538948
  89.4 9.7 %copy-start.5 = (f32[3,9,128,128]{3,2,1,0:T(8,128)S(1)}, f32[3,9,128,128]{3,2,1,0:T(8,128)}, u32[]{:S(2)}) copy-start(f32[3,9,128,128]{3,2,1,0:T(8,128)} %get-tuple-element.8) | copy-start | bytes 5308420

commit v3 on v1

--- a/solution.py
+++ b/solution.py
@@ -17,7 +17,7 @@
     n, line, cols, height, breadth, ch, tile, factor,
     vol, ker, grd,
     act_out, ing_out, dw_out,
-    vp, gp, wf, wb, xt, gs, acc, fin, r_sib, r_lo, r_hi, r_y, act, ing,
+    vp, gp, wf, wk, wb, xt, gs, acc, fin, r_sib, r_lo, r_hi, r_y, act, ing,
     s_in, s_w, s_hs, s_hr, s_sib, r_sibs, s_line, r_los, r_his, s_y, r_ys,
     s_up, s_dn, s_fs, r_fin, r_fsib, s_out,
 ):
@@ -49,11 +49,8 @@
     wloads = []
     for c in range(3):
         wloads.append(pltpu.make_async_copy(
-            ker.at[:, :, c], wf.at[:, :, :, pl.ds(c * ch, ch)], s_w.at[0, c]))
-    for a in range(3):
-        for b in range(3):
-            wloads.append(pltpu.make_async_copy(
-                ker.at[a, b], wb.at[:, :, pl.ds((8 - 3 * a - b) * ch, ch)], s_w.at[1 + a, b]))
+            ker.at[:, :, c], wf.at[:, :, :, pl.ds(c * ch, ch)], s_w.at[c]))
+    wloads.append(pltpu.make_async_copy(ker, wk, s_w.at[3]))
     for copy in wloads:
         copy.start()
 
@@ -180,18 +177,20 @@
                 bands.append(planes[d + a, at, :])
         lhs = jnp.concatenate(bands, axis=1)
         if backward:
-            rhs = jnp.concatenate([weights[c] for c in range(3)], axis=0)
-            sums = lax.dot_general(lhs, rhs, (((1,), (1,)), ((), ())), preferred_element_type=F32)
-            first, last = sums[:, 2 * ch:], sums[:, :ch]
+            rhs = weights[...]
         else:
             rhs = jnp.concatenate([weights[a, b] for a in range(3) for b in range(3)], axis=0)
-            sums = jnp.dot(lhs, rhs, preferred_element_type=F32)
-            first, last = sums[:, :ch], sums[:, 2 * ch:]
+        sums = jnp.dot(lhs, rhs, preferred_element_type=F32)
+        first, last = sums[:, :ch], sums[:, 2 * ch:]
         total = sums[:, ch:2 * ch] + before_of(first) + after_of(last)
         out[d, pl.ds(pl.multiple_of(start, 16), rows), :] = total.astype(BF16)
 
     for copy in wloads:
         copy.wait()
+    for a in range(3):
+        for b in range(3):
+            for c in range(3):
+                wb[pl.ds((3 * a + b) * ch, ch), pl.ds(c * ch, ch)] = wk[2 - a, 2 - b, 2 - c].T
 
     def inside_act(k, carry):
         conv_tile(vp, wf, act, inside, k, False)
@@ -341,26 +340,28 @@
             stage(j)
 
     lags = (
-        (6, stage_spread), (4, stage_across), (3, stage_root),
-        (2, stage_line), (1, stage_sibling), (0, stage_send),
+        (1, stage_sibling), (3, stage_line), (5, stage_root),
+        (7, stage_across), (10, stage_spread),
     )
-    steps = max(taps + 6, 2 * tiles)
+    steps = max(taps + 10, 2 * tiles)
 
     def step(s, carry):
+        during(s, stage_send)
+
+        @pl.when(s < tiles)
+        def _():
+            conv_tile(vp, wf, act, core, s, False)
+
+        @pl.when(s == tiles)
+        def _():
+            await_off(1, grd, gp)
+
+        @pl.when(jnp.logical_and(s >= tiles, s < 2 * tiles))
+        def _():
+            conv_tile(gp, wb, ing, core, s - tiles, True)
+
         for lag, stage in lags:
             during(s - lag, stage)
-
-        @pl.when(s < tiles)
-        def _():
-            conv_tile(vp, wf, act, core, s, False)
-
-        @pl.when(s == tiles)
-        def _():
-            await_off(1, grd, gp)
-
-        @pl.when(jnp.logical_and(s >= tiles, s < 2 * tiles))
-        def _():
-            conv_tile(gp, wb, ing, core, s - tiles, True)
         return carry
 
     lax.fori_loop(0, steps, step, 0)
@@ -408,6 +409,17 @@
     act_copy.wait()
     ing_copy.wait()
     dw_copy.wait()
+
+
+def results_kernel(act, ing, dw, act_out, ing_out, dw_out, sem):
+    copies = []
+    for src, dst in ((act, act_out), (ing, ing_out), (dw, dw_out)):
+        for k in range(src.shape[0]):
+            copies.append(pltpu.make_async_copy(src.at[k], dst.at[k], sem.at[len(copies)]))
+    for copy in copies:
+        copy.start()
+    for copy in copies:
+        copy.wait()
 
 
 def body(n, line, cols, volume, kernel, grad_out):
@@ -433,7 +445,8 @@
             pltpu.VMEM((4, cells + 2 * breadth, ch), BF16),
             pltpu.VMEM((4, cells + 2 * breadth, ch), BF16),
             pltpu.VMEM((3, 3, ch, 3 * ch), BF16),
-            pltpu.VMEM((3, ch, 9 * ch), BF16),
+            pltpu.VMEM((3, 3, 3, ch, ch), BF16),
+            pltpu.VMEM((9 * ch, 3 * ch), BF16),
             pltpu.VMEM((4 * ch, cells), BF16),
             pltpu.VMEM((3, 2, cells + 2 * breadth, ch), BF16),
             pltpu.VMEM((3, taps, ch, ch), F32),
@@ -444,7 +457,7 @@
             pltpu.VMEM((peers, taps, 3, half, ch), F32),
             pltpu.VMEM((planes, cells, ch), BF16),
             pltpu.VMEM((planes, cells, ch), BF16),
-            dma((4,)), dma((4, 3)), dma((2, 2)), dma((2, 2)),
+            dma((4,)), dma((4,)), dma((2, 2)), dma((2, 2)),
             dma((taps,)), dma((taps,)), dma((taps,)), dma((taps,)), dma((taps,)),
             dma((peers, taps)), dma((peers, taps)),
             dma((taps,)), dma((taps,)), dma((taps,)), dma((taps,)), dma((taps,)),
@@ -458,6 +471,15 @@
         kernel,
         grad_out.reshape(planes, cells, ch),
     )
+    outs = pl.pallas_call(
+        results_kernel,
+        out_shape=tuple(jax.ShapeDtypeStruct(o.shape, o.dtype) for o in outs),
+        in_specs=[pl.BlockSpec(memory_space=pl.ANY)] * 3,
+        out_specs=[pl.BlockSpec(memory_space=pl.ANY)] * 3,
+        scratch_shapes=[dma((7,))],
+        compiler_params=pltpu.CompilerParams(vmem_limit_bytes=56 * 1024 * 1024),
+        cost_estimate=pl.CostEstimate(flops=0, bytes_accessed=8_000_000, transcendentals=0),
+    )(*outs)
     activation = outs[0].reshape(volume.shape)
     input_grad = outs[1].reshape(volume.shape)
     return activation, input_grad, outs[2].reshape(3, 3, 3, ch, ch)

time: 89.4 us -> 198 us (2.21)
  Pallas kernels: 83 us -> 198 us
  local copies, waits for them, and re-layouts: 5.57 us -> 0 us
    pallas_call x0 -> x1, Pallas kernels: none -> 126 us  [body(): pl.pallas_call(results_kernel, out_shape=tuple((jax.ShapeDtypeStruct(o.sh...]
    pallas_call x1, Pallas kernels: 83 us -> 71.4 us  [body(): pl.pallas_call(functools.partial(layer_kernel, n, line, cols, height, bre...]
    unnamed x7 -> x0, local copies, waits for them, and re-layouts: 5.57 us -> none
where the time goes in v3:
time: 198 us
  Pallas kernels  198 us (100%)
    pallas_call x1, Pallas kernels, body(): pl.pallas_call(results_kernel, out_shape=tuple((jax.ShapeDtypeStruct(o.sh...  126 us
    pallas_call x1, Pallas kernels, body(): pl.pallas_call(functools.partial(layer_kernel, n, line, cols, height, bre...  71.4 us

profile of v3, /device:TPU:0, one launch (start us, length us, event | category | flops | bytes accessed | tf_op | source)
XLA Modules:
  0.0 198.3 jit_solution(10814403397884102603)
XLA Ops:
  0.6 71.4 %shard_map.58 = (bf16[2,2304,128]{2,1,0:T(8,128)(2,1)}, bf16[2,2304,128]{2,1,0:T(8,128)(2,1)}, f32[3,9,128,128]{3,2,1,0:T(8,128)}) custom-call(bf16[2,2304,128]{2,1,0:T(8,128)(2,1)} %bitcast.6, bf16[3,3,3,128,128]{4,3,2,1,0:T(8,128)(2,1)} %ker.1, bf16[2,2304,128]{2,1,0:T(8,128)(2,1)} %bitcast.7), custom_call_target="tpu_custom_call" | custom-call | flops 12230590464 | bytes 10000000 | tf_op jit(solution)/shard_map/pallas_call | solution.py:435
  72.0 126.2 %shard_map.59 = (bf16[2,2304,128]{2,1,0:T(8,128)(2,1)}, bf16[2,2304,128]{2,1,0:T(8,128)(2,1)}, f32[3,9,128,128]{3,2,1,0:T(8,128)}) custom-call(bf16[2,2304,128]{2,1,0:T(8,128)(2,1)} %get-tuple-element.9.act, bf16[2,2304,128]{2,1,0:T(8,128)(2,1)} %get-tuple-element.10.ing, f32[3,9,128,128]{3,2,1,0:T(8,128)} %get-tuple-element.11.dw), custom_call_target="tpu_custom_call" | custom-call | bytes 8000000 | tf_op jit(solution)/shard_map/pallas_call | solution.py:474

commit v4 on v3

--- a/solution.py
+++ b/solution.py
@@ -157,16 +157,13 @@
     await_sibling(0, vol, vp)
     transpose_planes(((1, 0), (2, 1), (slot_sib, 2)))
 
-    def own_part(t, carry):
+    def own_part(t):
         rhs = jnp.concatenate([grads(t, 0), grads(t, 1)], axis=1)
         full = jnp.dot(xt[pl.ds(0, 3 * ch), :], rhs, preferred_element_type=F32)
         beside = full[2 * ch:]
-        acc[0, t] = full[:ch, ch:] + jnp.where(core == 1, beside[:, :ch], 0.0)
-        acc[1, t] = full[:ch, :ch] + full[ch:2 * ch, ch:]
-        acc[2, t] = full[ch:2 * ch, :ch] + jnp.where(core == 0, beside[:, ch:], 0.0)
-        return carry
-
-    lax.fori_loop(0, taps, own_part, 0)
+        acc[t] = full[:ch, ch:] + jnp.where(core == 1, beside[:, :ch], 0.0)
+        acc[taps + t] = full[:ch, :ch] + full[ch:2 * ch, ch:]
+        acc[2 * taps + t] = full[ch:2 * ch, :ch] + jnp.where(core == 0, beside[:, ch:], 0.0)
 
     def conv_tile(planes, weights, out, d, k, backward):
         start = k * rows
@@ -185,68 +182,54 @@
         total = sums[:, ch:2 * ch] + before_of(first) + after_of(last)
         out[d, pl.ds(pl.multiple_of(start, 16), rows), :] = total.astype(BF16)
 
-    for copy in wloads:
-        copy.wait()
-    for a in range(3):
-        for b in range(3):
-            for c in range(3):
-                wb[pl.ds((3 * a + b) * ch, ch), pl.ds(c * ch, ch)] = wk[2 - a, 2 - b, 2 - c].T
-
-    def inside_act(k, carry):
-        conv_tile(vp, wf, act, inside, k, False)
-        return carry
-
-    def inside_ing(k, carry):
-        conv_tile(gp, wb, ing, inside, k, True)
-        return carry
-
-    lax.fori_loop(0, tiles, inside_act, 0)
-    await_sibling(1, grd, gp)
-    lax.fori_loop(0, tiles, inside_ing, 0)
-
-    await_off(0, vol, vp)
-
-    @pl.when(off_chip)
-    def _():
-        halo_off(1, grd, gp).start()
-
-    transpose_planes(((slot_off, 3),))
-
     mine = pl.ds(pl.multiple_of(core * half, half), half)
     other = pl.ds(pl.multiple_of((1 - core) * half, half), half)
 
     def root(j):
         return (line - 1) // 2 + lax.rem(j, 2) * (line // 2 - (line - 1) // 2)
 
+    def spot(j):
+        return lax.rem(j + taps, 3 * taps)
+
     def to_sibling(j):
-        return remote(acc.at[:, j, other], r_sib.at[j], s_sib.at[j], r_sibs.at[j], sib)
+        return remote(acc.at[spot(j), other], r_sib.at[j], s_sib.at[j], r_sibs.at[j], sib)
 
     def line_up(j):
-        return remote(acc.at[:, j, mine], r_lo.at[j], s_line.at[j], r_los.at[j], zhi)
+        return remote(acc.at[spot(j), mine], r_lo.at[j], s_line.at[j], r_los.at[j], zhi)
 
     def line_down(j):
-        return remote(acc.at[:, j, mine], r_hi.at[j], s_line.at[j], r_his.at[j], zlo)
+        return remote(acc.at[spot(j), mine], r_hi.at[j], s_line.at[j], r_his.at[j], zlo)
 
     def across(j, k):
-        return remote(acc.at[:, j, mine], r_y.at[k - 1, j], s_y.at[k - 1, j], r_ys.at[k - 1, j], peer(k))
+        return remote(acc.at[spot(j), mine], r_y.at[k - 1, j], s_y.at[k - 1, j], r_ys.at[k - 1, j], peer(k))
 
     def final_up(j):
-        return remote(fin.at[:, j, mine], fin.at[:, j, mine], s_up.at[j], r_fin.at[j], zhi)
+        return remote(fin.at[spot(j), mine], fin.at[spot(j), mine], s_up.at[j], r_fin.at[j], zhi)
 
     def final_down(j):
-        return remote(fin.at[:, j, mine], fin.at[:, j, mine], s_dn.at[j], r_fin.at[j], zlo)
+        return remote(fin.at[spot(j), mine], fin.at[spot(j), mine], s_dn.at[j], r_fin.at[j], zlo)
 
     def final_sibling(j):
-        return remote(fin.at[:, j, mine], fin.at[:, j, mine], s_fs.at[j], r_fsib.at[j], sib)
+        return remote(fin.at[spot(j), mine], fin.at[spot(j), mine], s_fs.at[j], r_fsib.at[j], sib)
 
     def stage_send(j):
-        part = jnp.dot(xt[pl.ds(3 * ch, ch), :], grads(j, core), preferred_element_type=F32)
-        acc[2 * core, j] = acc[2 * core, j] + part
+        @pl.when(j < taps)
+        def _():
+            own_part(j)
+
+        @pl.when(jnp.logical_or(
+            jnp.logical_and(core == 1, jnp.logical_and(j >= taps, j < 2 * taps)),
+            jnp.logical_and(core == 0, j >= 2 * taps)))
+        def _():
+            part = jnp.dot(
+                xt[pl.ds(3 * ch, ch), :], grads(lax.rem(j, taps), core), preferred_element_type=F32)
+            acc[spot(j)] = acc[spot(j)] + part
+
         to_sibling(j).start()
 
     def stage_sibling(j):
         to_sibling(j).wait_recv()
-        acc[:, j, mine, :] = acc[:, j, mine, :] + r_sib[j]
+        acc[spot(j), mine, :] = acc[spot(j), mine, :] + r_sib[j]
 
         @pl.when(jnp.logical_and(z == 0, root(j) != 0))
         def _():
@@ -260,13 +243,13 @@
         @pl.when(jnp.logical_and(z > 0, z < root(j)))
         def _():
             line_up(j).wait_recv()
-            acc[:, j, mine, :] = acc[:, j, mine, :] + r_lo[j]
+            acc[spot(j), mine, :] = acc[spot(j), mine, :] + r_lo[j]
             line_up(j).start()
 
         @pl.when(jnp.logical_and(z < line - 1, z > root(j)))
         def _():
             line_down(j).wait_recv()
-            acc[:, j, mine, :] = acc[:, j, mine, :] + r_hi[j]
+            acc[spot(j), mine, :] = acc[spot(j), mine, :] + r_hi[j]
             line_down(j).start()
 
     def stage_root(j):
@@ -275,12 +258,12 @@
             @pl.when(has_lo)
             def _():
                 line_up(j).wait_recv()
-                acc[:, j, mine, :] = acc[:, j, mine, :] + r_lo[j]
+                acc[spot(j), mine, :] = acc[spot(j), mine, :] + r_lo[j]
 
             @pl.when(has_hi)
             def _():
                 line_down(j).wait_recv()
-                acc[:, j, mine, :] = acc[:, j, mine, :] + r_hi[j]
+                acc[spot(j), mine, :] = acc[spot(j), mine, :] + r_hi[j]
 
             for k in range(1, cols):
                 across(j, k).start()
@@ -291,17 +274,17 @@
             for k in range(1, cols):
                 across(j, k).wait_recv()
             if cols <= 2:
-                total = acc[:, j, mine, :]
+                total = acc[spot(j), mine, :]
                 for k in range(1, cols):
                     total = total + r_y[k - 1, j]
             else:
-                total = jnp.zeros((3, half, ch), F32)
+                total = jnp.zeros((half, ch), F32)
                 for i in range(cols):
-                    term = acc[:, j, mine, :]
+                    term = acc[spot(j), mine, :]
                     for k in range(1, cols):
                         term = jnp.where(lax.rem(y + cols - k, cols) == i, r_y[k - 1, j], term)
                     total = total + term
-            fin[:, j, mine, :] = total * factor
+            fin[spot(j), mine, :] = total * factor
 
             @pl.when(has_lo)
             def _():
@@ -334,31 +317,78 @@
 
             final_sibling(j).start()
 
-    def during(j, stage):
-        @pl.when(jnp.logical_and(j >= 0, j < taps))
-        def _():
-            stage(j)
+    begin_act, begin_ing, begin_halo = taps, taps + tiles, taps + 2 * tiles
+    end_halo = begin_halo + 2 * taps
+    gap = begin_halo - taps
+
+    def during(at, stage):
+        first = jnp.logical_and(at >= 0, at < taps)
+        second = jnp.logical_and(at >= begin_halo, at < end_halo)
+
+        @pl.when(jnp.logical_or(first, second))
+        def _():
+            stage(at - gap * (at >= begin_halo).astype(jnp.int32))
+
+    def spread_near(j):
+        @pl.when(jnp.logical_and(z >= root(j) - 1, z <= root(j) + 1))
+        def _():
+            stage_spread(j)
+
+    def spread_far(j):
+        @pl.when(jnp.logical_or(z < root(j) - 1, z > root(j) + 1))
+        def _():
+            stage_spread(j)
 
     lags = (
-        (1, stage_sibling), (3, stage_line), (5, stage_root),
-        (7, stage_across), (10, stage_spread),
+        (2, stage_sibling), (5, stage_line), (8, stage_root),
+        (11, stage_across), (14, spread_near), (17, spread_far),
     )
-    steps = max(taps + 10, 2 * tiles)
+    steps = end_halo + 17
 
     def step(s, carry):
+        late = (s >= begin_halo).astype(jnp.int32)
+        plane = inside + late * (core - inside)
+
+        @pl.when(s == begin_halo)
+        def _():
+            await_off(0, vol, vp)
+
+            @pl.when(off_chip)
+            def _():
+                halo_off(1, grd, gp).start()
+
+            transpose_planes(((slot_off, 3),))
+
         during(s, stage_send)
 
-        @pl.when(s < tiles)
-        def _():
-            conv_tile(vp, wf, act, core, s, False)
-
-        @pl.when(s == tiles)
+        @pl.when(s == begin_act)
+        def _():
+            for copy in wloads:
+                copy.wait()
+
+        @pl.when(jnp.logical_or(
+            jnp.logical_and(s >= begin_act, s < begin_ing),
+            jnp.logical_and(s >= begin_halo, s < begin_halo + tiles)))
+        def _():
+            conv_tile(vp, wf, act, plane, s - begin_act - late * (begin_halo - begin_act), False)
+
+        @pl.when(s == begin_ing)
+        def _():
+            for a in range(3):
+                for b in range(3):
+                    for c in range(3):
+                        wb[pl.ds((3 * a + b) * ch, ch), pl.ds(c * ch, ch)] = wk[2 - a, 2 - b, 2 - c].T
+            await_sibling(1, grd, gp)
+
+        @pl.when(s == end_halo)
         def _():
             await_off(1, grd, gp)
 
-        @pl.when(jnp.logical_and(s >= tiles, s < 2 * tiles))
-        def _():
-            conv_tile(gp, wb, ing, core, s - tiles, True)
+        @pl.when(jnp.logical_or(
+            jnp.logical_and(s >= begin_ing, s < begin_halo),
+            jnp.logical_and(s >= end_halo, s < end_halo + tiles)))
+        def _():
+            conv_tile(gp, wb, ing, plane, s - begin_ing - late * (end_halo - begin_ing), True)
 
         for lag, stage in lags:
             during(s - lag, stage)
@@ -396,7 +426,7 @@
         final_sibling(j).wait_recv()
         return carry
 
-    lax.fori_loop(0, taps, finish, 0)
+    lax.fori_loop(0, 3 * taps, finish, 0)
     dw_copy.start()
 
     for which, src, dst in ((0, vol, vp), (1, grd, gp)):
@@ -411,22 +441,17 @@
     dw_copy.wait()
 
 
-def results_kernel(act, ing, dw, act_out, ing_out, dw_out, sem):
-    copies = []
-    for src, dst in ((act, act_out), (ing, ing_out), (dw, dw_out)):
-        for k in range(src.shape[0]):
-            copies.append(pltpu.make_async_copy(src.at[k], dst.at[k], sem.at[len(copies)]))
-    for copy in copies:
-        copy.start()
-    for copy in copies:
-        copy.wait()
+def results_kernel(act, ing, dw, act_out, ing_out, dw_out):
+    act_out[...] = act[...]
+    ing_out[...] = ing[...]
+    dw_out[...] = dw[...]
 
 
 def body(n, line, cols, volume, kernel, grad_out):
     planes, height, breadth, ch = volume.shape
     cells = height * breadth
     half = ch // 2
-    taps = 9
+    chunks = 27
     tile = 8
     factor = float(np.float32(1.0) / np.sqrt(np.float32(n * planes * cells)))
     dma = pltpu.SemaphoreType.DMA
@@ -437,7 +462,7 @@
         out_shape=(
             jax.ShapeDtypeStruct((planes, cells, ch), BF16),
             jax.ShapeDtypeStruct((planes, cells, ch), BF16),
-            jax.ShapeDtypeStruct((3, taps, ch, ch), F32),
+            jax.ShapeDtypeStruct((chunks, ch, ch), F32),
         ),
         in_specs=[pl.BlockSpec(memory_space=pl.ANY)] * 3,
         out_specs=[pl.BlockSpec(memory_space=pl.ANY)] * 3,
@@ -449,18 +474,18 @@
             pltpu.VMEM((9 * ch, 3 * ch), BF16),
             pltpu.VMEM((4 * ch, cells), BF16),
             pltpu.VMEM((3, 2, cells + 2 * breadth, ch), BF16),
-            pltpu.VMEM((3, taps, ch, ch), F32),
-            pltpu.VMEM((3, taps, ch, ch), F32),
-            pltpu.VMEM((taps, 3, half, ch), F32),
-            pltpu.VMEM((taps, 3, half, ch), F32),
-            pltpu.VMEM((taps, 3, half, ch), F32),
-            pltpu.VMEM((peers, taps, 3, half, ch), F32),
+            pltpu.VMEM((chunks, ch, ch), F32),
+            pltpu.VMEM((chunks, ch, ch), F32),
+            pltpu.VMEM((chunks, half, ch), F32),
+            pltpu.VMEM((chunks, half, ch), F32),
+            pltpu.VMEM((chunks, half, ch), F32),
+            pltpu.VMEM((peers, chunks, half, ch), F32),
             pltpu.VMEM((planes, cells, ch), BF16),
             pltpu.VMEM((planes, cells, ch), BF16),
             dma((4,)), dma((4,)), dma((2, 2)), dma((2, 2)),
-            dma((taps,)), dma((taps,)), dma((taps,)), dma((taps,)), dma((taps,)),
-            dma((peers, taps)), dma((peers, taps)),
-            dma((taps,)), dma((taps,)), dma((taps,)), dma((taps,)), dma((taps,)),
+            dma((chunks,)), dma((chunks,)), dma((chunks,)), dma((chunks,)), dma((chunks,)),
+            dma((peers, chunks)), dma((peers, chunks)),
+            dma((chunks,)), dma((chunks,)), dma((chunks,)), dma((chunks,)), dma((chunks,)),
             dma((3,)),
         ],
         compiler_params=pltpu.CompilerParams(
@@ -471,15 +496,19 @@
         kernel,
         grad_out.reshape(planes, cells, ch),
     )
+    parts = 6
+    pieces = [
+        outs[0].reshape(parts, -1, ch), outs[1].reshape(parts, -1, ch), outs[2].reshape(parts, -1, ch)]
+    blocks = [pl.BlockSpec((1, piece.shape[1], ch), lambda i: (i, 0, 0)) for piece in pieces]
     outs = pl.pallas_call(
         results_kernel,
-        out_shape=tuple(jax.ShapeDtypeStruct(o.shape, o.dtype) for o in outs),
-        in_specs=[pl.BlockSpec(memory_space=pl.ANY)] * 3,
-        out_specs=[pl.BlockSpec(memory_space=pl.ANY)] * 3,
-        scratch_shapes=[dma((7,))],
+        grid=(parts,),
+        out_shape=[jax.ShapeDtypeStruct(piece.shape, piece.dtype) for piece in pieces],
+        in_specs=blocks,
+        out_specs=blocks,
         compiler_params=pltpu.CompilerParams(vmem_limit_bytes=56 * 1024 * 1024),
         cost_estimate=pl.CostEstimate(flops=0, bytes_accessed=8_000_000, transcendentals=0),
-    )(*outs)
+    )(*pieces)
     activation = outs[0].reshape(volume.shape)
     input_grad = outs[1].reshape(volume.shape)
     return activation, input_grad, outs[2].reshape(3, 3, 3, ch, ch)

time: 198 us -> 81.6 us (0.41)
  Pallas kernels: 198 us -> 80.7 us
    pallas_call x1, Pallas kernels: 126 us -> 5.79 us  [body(): pl.pallas_call(results_kernel, grid=(parts,), out_shape=[jax.ShapeDtypeSt...]
    pallas_call x1, Pallas kernels: 71.4 us -> 75 us  [body(): pl.pallas_call(functools.partial(layer_kernel, n, line, cols, height, bre...]
where the time goes in v4:
time: 81.6 us; the launch traced here: 81.4 us
  Pallas kernels  80.7 us (99%)
    pallas_call x1, Pallas kernels, body(): pl.pallas_call(functools.partial(layer_kernel, n, line, cols, height, bre...  75 us
    pallas_call x1, Pallas kernels, body(): pl.pallas_call(results_kernel, grid=(parts,), out_shape=[jax.ShapeDtypeSt...  5.79 us

profile of v4, /device:TPU:0, one launch (start us, length us, event | category | flops | bytes accessed | tf_op | source)
XLA Modules:
  0.0 81.4 jit_solution(11070768223335640227)
XLA Ops:
  0.6 75.0 %shard_map.58 = (bf16[2,2304,128]{2,1,0:T(8,128)(2,1)}, bf16[2,2304,128]{2,1,0:T(8,128)(2,1)}, f32[27,128,128]{2,1,0:T(8,128)}) custom-call(bf16[2,2304,128]{2,1,0:T(8,128)(2,1)} %bitcast.12, bf16[3,3,3,128,128]{4,3,2,1,0:T(8,128)(2,1)} %ker.1, bf16[2,2304,128]{2,1,0:T(8,128)(2,1)} %bitcast.13), custom_call_target="tpu_custom_call" | custom-call | flops 12230590464 | bytes 10000000 | tf_op jit(solution)/shard_map/pallas_call | solution.py:460
  75.6 5.8 %shard_map.59 = (bf16[6,768,128]{2,1,0:T(8,128)(2,1)}, bf16[6,768,128]{2,1,0:T(8,128)(2,1)}, f32[6,576,128]{2,1,0:T(8,128)}) custom-call(bf16[6,768,128]{2,1,0:T(8,128)(2,1)} %bitcast.9, bf16[6,768,128]{2,1,0:T(8,128)(2,1)} %bitcast.10, f32[6,576,128]{2,1,0:T(8,128)} %bitcast.8), custom_call_target="tpu_custom_call" | custom-call | bytes 8000000 | tf_op jit(solution)/shard_map/pallas_call | solution.py:503

commit v5 on v4

--- a/solution.py
+++ b/solution.py
@@ -80,26 +80,31 @@
     inside = 1 - core
     slot_sib, slot_off = 3 * inside, 3 * core
 
-    def halo_sibling(which, src, dst):
-        return remote(src.at[inside], dst.at[3 * core, inner], s_hs.at[which, 0], s_hr.at[which, 0], sib)
-
-    def halo_off(which, src, dst):
-        return remote(src.at[core], dst.at[3 * inside, inner], s_hs.at[which, 1], s_hr.at[which, 1], off_dev)
-
-    def await_sibling(which, src, dst):
-        remote(src.at[inside], dst.at[slot_sib, inner], s_hs.at[which, 0], s_hr.at[which, 0], sib).wait_recv()
-
-    def await_off(which, src, dst):
+    def halo_sibling(which, dst):
+        return remote(dst.at[1 + inside, inner], dst.at[3 * core, inner], s_hs.at[which, 0], s_hr.at[which, 0], sib)
+
+    def halo_off(which, dst):
+        return remote(dst.at[1 + core, inner], dst.at[3 * inside, inner], s_hs.at[which, 1], s_hr.at[which, 1], off_dev)
+
+    def await_sibling(which, dst):
+        remote(dst.at[1 + inside, inner], dst.at[slot_sib, inner], s_hs.at[which, 0], s_hr.at[which, 0], sib).wait_recv()
+
+    def await_off(which, dst):
         @pl.when(off_chip)
         def _():
-            remote(src.at[core], dst.at[slot_off, inner], s_hs.at[which, 1], s_hr.at[which, 1], off_dev).wait_recv()
+            remote(dst.at[1 + core, inner], dst.at[slot_off, inner], s_hs.at[which, 1], s_hr.at[which, 1], off_dev).wait_recv()
+
+    for copy in loads[:2]:
+        copy.wait()
 
     @pl.when(off_chip)
     def _():
-        halo_off(0, vol, vp).start()
-
-    halo_sibling(0, vol, vp).start()
-    halo_sibling(1, grd, gp).start()
+        halo_off(0, vp).start()
+
+    halo_sibling(0, vp).start()
+    for copy in loads[2:]:
+        copy.wait()
+    halo_sibling(1, gp).start()
 
     edge = jnp.zeros((breadth, ch), BF16)
     for ref in (vp, gp):
@@ -126,9 +131,6 @@
     def after_of(v):
         return jnp.where(column == breadth - 1, 0.0, pltpu.roll(v, rows - 1, 0))
 
-    for copy in loads:
-        copy.wait()
-
     def shift_tile(k, carry):
         at = pl.ds(pl.multiple_of(breadth + k * rows, 16), rows)
         for d in range(2):
@@ -154,7 +156,7 @@
         b, c = t // 3, lax.rem(t, 3)
         return gs[c, d, pl.ds(pl.multiple_of((2 - b) * breadth, 16), cells), :]
 
-    await_sibling(0, vol, vp)
+    await_sibling(0, vp)
     transpose_planes(((1, 0), (2, 1), (slot_sib, 2)))
 
     def own_part(t):
@@ -351,11 +353,11 @@
 
         @pl.when(s == begin_halo)
         def _():
-            await_off(0, vol, vp)
+            await_off(0, vp)
 
             @pl.when(off_chip)
             def _():
-                halo_off(1, grd, gp).start()
+                halo_off(1, gp).start()
 
             transpose_planes(((slot_off, 3),))
 
@@ -378,11 +380,11 @@
                 for b in range(3):
                     for c in range(3):
                         wb[pl.ds((3 * a + b) * ch, ch), pl.ds(c * ch, ch)] = wk[2 - a, 2 - b, 2 - c].T
-            await_sibling(1, grd, gp)
+            await_sibling(1, gp)
 
         @pl.when(s == end_halo)
         def _():
-            await_off(1, grd, gp)
+            await_off(1, gp)
 
         @pl.when(jnp.logical_or(
             jnp.logical_and(s >= begin_ing, s < begin_halo),
@@ -429,22 +431,16 @@
     lax.fori_loop(0, 3 * taps, finish, 0)
     dw_copy.start()
 
-    for which, src, dst in ((0, vol, vp), (1, grd, gp)):
-        halo_sibling(which, src, dst).wait_send()
+    for which, dst in ((0, vp), (1, gp)):
+        halo_sibling(which, dst).wait_send()
 
         @pl.when(off_chip)
-        def _(which=which, src=src, dst=dst):
-            halo_off(which, src, dst).wait_send()
+        def _(which=which, dst=dst):
+            halo_off(which, dst).wait_send()
 
     act_copy.wait()
     ing_copy.wait()
     dw_copy.wait()
-
-
-def results_kernel(act, ing, dw, act_out, ing_out, dw_out):
-    act_out[...] = act[...]
-    ing_out[...] = ing[...]
-    dw_out[...] = dw[...]
 
 
 def body(n, line, cols, volume, kernel, grad_out):
@@ -489,26 +485,13 @@
             dma((3,)),
         ],
         compiler_params=pltpu.CompilerParams(
-            collective_id=0, has_side_effects=True, vmem_limit_bytes=56 * 1024 * 1024),
+            collective_id=0, has_side_effects=True, vmem_limit_bytes=(24 + peers) * 1024 * 1024),
         cost_estimate=pl.CostEstimate(flops=flops, bytes_accessed=10_000_000, transcendentals=0),
     )(
         volume.reshape(planes, cells, ch),
         kernel,
         grad_out.reshape(planes, cells, ch),
     )
-    parts = 6
-    pieces = [
-        outs[0].reshape(parts, -1, ch), outs[1].reshape(parts, -1, ch), outs[2].reshape(parts, -1, ch)]
-    blocks = [pl.BlockSpec((1, piece.shape[1], ch), lambda i: (i, 0, 0)) for piece in pieces]
-    outs = pl.pallas_call(
-        results_kernel,
-        grid=(parts,),
-        out_shape=[jax.ShapeDtypeStruct(piece.shape, piece.dtype) for piece in pieces],
-        in_specs=blocks,
-        out_specs=blocks,
-        compiler_params=pltpu.CompilerParams(vmem_limit_bytes=56 * 1024 * 1024),
-        cost_estimate=pl.CostEstimate(flops=0, bytes_accessed=8_000_000, transcendentals=0),
-    )(*pieces)
     activation = outs[0].reshape(volume.shape)
     input_grad = outs[1].reshape(volume.shape)
     return activation, input_grad, outs[2].reshape(3, 3, 3, ch, ch)

time: 81.6 us -> 82.3 us (level)
  local copies, waits for them, and re-layouts: 0 us -> 6.94 us
  Pallas kernels: 80.7 us -> 74.4 us
    unnamed x0 -> x9, local copies, waits for them, and re-layouts: none -> 6.94 us
    pallas_call x1 -> x0, Pallas kernels: 5.79 us -> none  [body(): pl.pallas_call(results_kernel, grid=(parts,), out_shape=[jax.ShapeDtypeSt...]
where the time goes in v5:
time: 82.3 us; the launch traced here: 82 us
  Pallas kernels  74.4 us (90%)
  local copies, waits for them, and re-layouts  6.94 us (8%)
    pallas_call x1, Pallas kernels, body(): pl.pallas_call(functools.partial(layer_kernel, n, line, cols, height, bre...  74.4 us
    unnamed x9, local copies, waits for them, and re-layouts  6.94 us

profile of v5, /device:TPU:0, one launch (start us, length us, event | category | flops | bytes accessed | tf_op | source)
XLA Modules:
  0.0 82.0 jit_solution(2862966333779741259)
XLA Ops:
  0.6 0.0 copy-start
  0.6 1.3 %copy-done = bf16[2,48,48,128]{3,2,1,0:T(8,128)(2,1)S(1)} copy-done((bf16[2,48,48,128]{3,2,1,0:T(8,128)(2,1)S(1)}, bf16[2,48,48,128]{3,2,1,0:T(8,128)(2,1)}, u32[]{:S(2)}) %copy-start) | copy-done | bytes 1179672
  1.9 0.0 copy-start.1
  1.9 1.3 %copy-done.1 = bf16[2,48,48,128]{3,2,1,0:T(8,128)(2,1)S(1)} copy-done((bf16[2,48,48,128]{3,2,1,0:T(8,128)(2,1)S(1)}, bf16[2,48,48,128]{3,2,1,0:T(8,128)(2,1)}, u32[]{:S(2)}) %copy-start.1) | copy-done | bytes 1179672
  3.2 0.0 copy-start.2
  3.2 1.2 %copy-done.2 = bf16[3,3,3,128,128]{4,3,2,1,0:T(8,128)(2,1)S(1)} copy-done((bf16[3,3,3,128,128]{4,3,2,1,0:T(8,128)(2,1)S(1)}, bf16[3,3,3,128,128]{4,3,2,1,0:T(8,128)(2,1)}, u32[]{:S(2)}) %copy-start.2) | copy-done | bytes 884760
  4.3 74.4 %shard_map.58 = (bf16[2,2304,128]{2,1,0:T(8,128)(2,1)S(1)}, bf16[2,2304,128]{2,1,0:T(8,128)(2,1)S(1)}, f32[27,128,128]{2,1,0:T(8,128)S(1)}) custom-call(bf16[2,2304,128]{2,1,0:T(8,128)(2,1)S(1)} %bitcast.8, bf16[3,3,3,128,128]{4,3,2,1,0:T(8,128)(2,1)S(1)} %copy-done.2, bf16[2,2304,128]{2,1,0:T(8,128)(2,1)S(1)} %bitcast.9), custom_call_target="tpu_custom_call" | custom-call | flops 12230590464 | bytes 10000000 | tf_op jit(solution)/shard_map/pallas_call | solution.py:456
  78.8 1.0 %copy.9 = bf16[2,48,48,128]{3,2,1,0:T(8,128)(2,1)} copy(bf16[2,48,48,128]{3,2,1,0:T(8,128)(2,1)S(1)} %bitcast.7) | data formatting | bytes 2359296
  79.8 1.0 %copy.10 = bf16[2,48,48,128]{3,2,1,0:T(8,128)(2,1)} copy(bf16[2,48,48,128]{3,2,1,0:T(8,128)(2,1)S(1)} %bitcast.6) | data formatting | bytes 2359296
  80.8 1.2 %copy.11 = f32[3,3,3,128,128]{4,3,2,1,0:T(8,128)} copy(f32[3,3,3,128,128]{4,3,2,1,0:T(8,128)S(1)} %bitcast.5) | data formatting | bytes 3538944
Async XLA Ops:
  0.6 1.3 %copy-start = (bf16[2,48,48,128]{3,2,1,0:T(8,128)(2,1)S(1)}, bf16[2,48,48,128]{3,2,1,0:T(8,128)(2,1)}, u32[]{:S(2)}) copy-start(bf16[2,48,48,128]{3,2,1,0:T(8,128)(2,1)} %param.3) | copy-start | bytes 3538948
  1.9 1.3 %copy-start.1 = (bf16[2,48,48,128]{3,2,1,0:T(8,128)(2,1)S(1)}, bf16[2,48,48,128]{3,2,1,0:T(8,128)(2,1)}, u32[]{:S(2)}) copy-start(bf16[2,48,48,128]{3,2,1,0:T(8,128)(2,1)} %param.5) | copy-start | bytes 3538948
  3.2 1.2 %copy-start.2 = (bf16[3,3,3,128,128]{4,3,2,1,0:T(8,128)(2,1)S(1)}, bf16[3,3,3,128,128]{4,3,2,1,0:T(8,128)(2,1)}, u32[]{:S(2)}) copy-start(bf16[3,3,3,128,128]{4,3,2,1,0:T(8,128)(2,1)} %ker.1) | copy-start | bytes 2654212

commit v6 on v3

--- a/solution.py
+++ b/solution.py
@@ -101,6 +101,10 @@
     halo_sibling(0, vol, vp).start()
     halo_sibling(1, grd, gp).start()
 
+    @pl.when(off_chip)
+    def _():
+        halo_off(1, grd, gp).start()
+
     edge = jnp.zeros((breadth, ch), BF16)
     for ref in (vp, gp):
         for p in range(4):
@@ -206,10 +210,6 @@
 
     await_off(0, vol, vp)
 
-    @pl.when(off_chip)
-    def _():
-        halo_off(1, grd, gp).start()
-
     transpose_planes(((slot_off, 3),))
 
     mine = pl.ds(pl.multiple_of(core * half, half), half)
@@ -409,17 +409,6 @@
     act_copy.wait()
     ing_copy.wait()
     dw_copy.wait()
-
-
-def results_kernel(act, ing, dw, act_out, ing_out, dw_out, sem):
-    copies = []
-    for src, dst in ((act, act_out), (ing, ing_out), (dw, dw_out)):
-        for k in range(src.shape[0]):
-            copies.append(pltpu.make_async_copy(src.at[k], dst.at[k], sem.at[len(copies)]))
-    for copy in copies:
-        copy.start()
-    for copy in copies:
-        copy.wait()
 
 
 def body(n, line, cols, volume, kernel, grad_out):
@@ -471,15 +460,6 @@
         kernel,
         grad_out.reshape(planes, cells, ch),
     )
-    outs = pl.pallas_call(
-        results_kernel,
-        out_shape=tuple(jax.ShapeDtypeStruct(o.shape, o.dtype) for o in outs),
-        in_specs=[pl.BlockSpec(memory_space=pl.ANY)] * 3,
-        out_specs=[pl.BlockSpec(memory_space=pl.ANY)] * 3,
-        scratch_shapes=[dma((7,))],
-        compiler_params=pltpu.CompilerParams(vmem_limit_bytes=56 * 1024 * 1024),
-        cost_estimate=pl.CostEstimate(flops=0, bytes_accessed=8_000_000, transcendentals=0),
-    )(*outs)
     activation = outs[0].reshape(volume.shape)
     input_grad = outs[1].reshape(volume.shape)
     return activation, input_grad, outs[2].reshape(3, 3, 3, ch, ch)

time: 198 us -> 76.2 us (0.38)
  Pallas kernels: 198 us -> 69.8 us
  local copies, waits for them, and re-layouts: 0 us -> 5.57 us
    pallas_call x1 -> x0, Pallas kernels: 126 us -> none  [body(): pl.pallas_call(results_kernel, out_shape=tuple((jax.ShapeDtypeStruct(o.sh...]
    unnamed x0 -> x7, local copies, waits for them, and re-layouts: none -> 5.57 us
where the time goes in v6:
time: 76.2 us; the launch traced here: 76 us
  Pallas kernels  69.8 us (92%)
  local copies, waits for them, and re-layouts  5.57 us (7%)
    pallas_call x1, Pallas kernels, body(): pl.pallas_call(functools.partial(layer_kernel, n, line, cols, height, bre...  69.8 us
    unnamed x7, local copies, waits for them, and re-layouts  5.57 us

profile of v6, /device:TPU:0, one launch (start us, length us, event | category | flops | bytes accessed | tf_op | source)
XLA Modules:
  0.0 76.0 jit_solution(12842791480511466259)
XLA Ops:
  0.6 69.8 %shard_map.58 = (bf16[2,2304,128]{2,1,0:T(8,128)(2,1)}, bf16[2,2304,128]{2,1,0:T(8,128)(2,1)}, f32[3,9,128,128]{3,2,1,0:T(8,128)}) custom-call(bf16[2,2304,128]{2,1,0:T(8,128)(2,1)} %bitcast.8, bf16[3,3,3,128,128]{4,3,2,1,0:T(8,128)(2,1)} %ker.1, bf16[2,2304,128]{2,1,0:T(8,128)(2,1)} %bitcast.9), custom_call_target="tpu_custom_call" | custom-call | flops 12230590464 | bytes 10000000 | tf_op jit(solution)/shard_map/pallas_call | solution.py:424
  70.4 0.0 copy-start.1
  70.4 2.5 %copy.9 = bf16[2,48,48,128]{3,2,1,0:T(8,128)(2,1)} copy(bf16[2,48,48,128]{3,2,1,0:T(8,128)(2,1)} %bitcast.7) | data formatting | bytes 2359296
  72.9 0.0 copy-done.1
  72.9 0.0 copy-start
  72.9 1.0 %copy.10 = bf16[2,48,48,128]{3,2,1,0:T(8,128)(2,1)} copy(bf16[2,48,48,128]{3,2,1,0:T(8,128)(2,1)S(1)} %bitcast.6) | data formatting | bytes 2359296
  73.9 0.9 %copy-done = f32[3,9,128,128]{3,2,1,0:T(8,128)S(1)} copy-done((f32[3,9,128,128]{3,2,1,0:T(8,128)S(1)}, f32[3,9,128,128]{3,2,1,0:T(8,128)}, u32[]{:S(2)}) %copy-start) | copy-done | bytes 1769496
  74.8 1.2 %copy.11 = f32[3,3,3,128,128]{4,3,2,1,0:T(8,128)} copy(f32[3,3,3,128,128]{4,3,2,1,0:T(8,128)S(1)} %bitcast.5) | data formatting | bytes 3538944
Async XLA Ops:
  70.4 2.5 %copy-start.1 = (bf16[2,2304,128]{2,1,0:T(8,128)(2,1)S(1)}, bf16[2,2304,128]{2,1,0:T(8,128)(2,1)}, u32[]{:S(2)}) copy-start(bf16[2,2304,128]{2,1,0:T(8,128)(2,1)} %get-tuple-element.7) | copy-start | bytes 3538948
  72.9 1.9 %copy-start = (f32[3,9,128,128]{3,2,1,0:T(8,128)S(1)}, f32[3,9,128,128]{3,2,1,0:T(8,128)}, u32[]{:S(2)}) copy-start(f32[3,9,128,128]{3,2,1,0:T(8,128)} %get-tuple-element.8) | copy-start | bytes 5308420
